TPU v7x, 32 devices: a whole 2x2x4 slice. The times are simulated.
32 devices in a mesh: tile: 16 (over z, y, core), scan: 2 (over x).
Axes of the slice: x: 2, y: 2, z: 4, core: 2. Of those that a mesh axis runs over, the one named last changes fastest.
Arguments:
- object_slab: float32 [2, 2, 1024, 512], P(None, None, 'tile', 'scan'), may hold values from -6 to 6
- probe_wave: bfloat16 [2, 512, 512], P(None, None, 'scan'), may hold values from -6 to 6
- amplitudes: float32 [32, 512, 512], P('tile', 'scan'), may hold values from 0.2 to 2
- row_offsets: int32 [32], P('tile'), may hold values from 0 to 63
- position_counts: int32 [16], P('tile'), may hold values from 0 to 2, as said below
Outputs:
- object_grad: float32 [2, 2, 1024, 512], P(None, None, 'tile', 'scan')
Inputs may be any that keep to these rules, and one draw needn't show every extreme that they name: position_counts is 1 to 2 on the first 8 tiles, equal to 2 on at least one of them, and 0 on the last 8 tiles.
All inputs are finite; a program needn't handle non-finite values.
Results may differ from a plain program's by a relative error of at most 0.0065.
Values may be sent and summed in bfloat16 or wider, within the bound.
No kernel may reach another device: no remote copies, remote signals or barrier semaphores. Data moves between devices by JAX's collectives and lax.ppermute only.
A program may use at most 64 MiB of HBM per device.

v0:
```python
import functools
import math

import jax
import jax.numpy as jnp
import ml_dtypes
import numpy as np
from jax import lax
from jax.experimental import pallas as pl
from jax.experimental.pallas import tpu as pltpu
from jax.sharding import PartitionSpec as P

fresnel = 0.5
smooth = 1.0
bf16 = jnp.bfloat16
f32 = jnp.float32


def tables(size):
    index = np.arange(size)
    angles = 2.0 * np.pi / size * (index[:, None] * index[None, :] % size)
    base = np.exp(1j * angles)
    far = np.conj(base) / math.sqrt(size)
    centred = np.where(index < size // 2, index, index - size).astype(np.float64)
    kernel = np.exp(-1j * np.pi * fresnel / size * centred * centred)
    near = (base * kernel[None, :]) @ np.conj(base).T / size

    def parts(table):
        stacked = np.stack([table.real, table.imag, -table.imag])
        return jnp.asarray(stacked.astype(ml_dtypes.bfloat16))

    return parts(far), parts(near)


def left(table, conjugate, wave, size):
    plus, minus = (1, 2) if not conjugate else (2, 1)
    top = jnp.concatenate([table[0], table[minus]], axis=1)
    bottom = jnp.concatenate([table[plus], table[0]], axis=1)
    real = jnp.dot(top, wave, preferred_element_type=f32)
    imag = jnp.dot(bottom, wave, preferred_element_type=f32)
    return real, imag


def right(table, conjugate, wave, size):
    plus, minus = (1, 2) if not conjugate else (2, 1)
    real_side = jnp.concatenate([table[0], table[minus]], axis=0)
    imag_side = jnp.concatenate([table[plus], table[0]], axis=0)
    real = jnp.dot(wave, real_side, preferred_element_type=f32)
    imag = jnp.dot(wave, imag_side, preferred_element_type=f32)
    return real, imag


def roll_kernel(size, meta, far, *refs):
    pieces, (probe_out, near_side, far_side) = refs[:-3], refs[-3:]
    offset, slot = meta[0], meta[2]
    row = lax.broadcasted_iota(jnp.int32, (size, size), 0)
    col = lax.broadcasted_iota(jnp.int32, (size, size), 1)
    gap = row - col - offset
    down = jnp.where((gap == 0) | (gap == -size), 1.0, 0.0).astype(bf16)
    gap = col - row - offset
    across = jnp.where((gap == 0) | (gap == -size), 1.0, 0.0).astype(bf16)
    for c in range(3):
        near_side[c] = jnp.dot(far[c], across, preferred_element_type=f32).astype(bf16)
        far_side[c] = jnp.dot(down, far[c], preferred_element_type=f32).astype(bf16)
    for c in range(2):
        done = 0
        for piece in pieces:
            turned = jnp.dot(down, piece[c], preferred_element_type=f32).astype(bf16)
            width = turned.shape[1]
            if len(pieces) == 2:
                at = pl.multiple_of(jnp.where(slot == done, 0, width), width)
                probe_out[c, :, pl.ds(at, width)] = turned
                done += 1
            else:
                probe_out[c, :, done : done + width] = turned
                done += width


def rolled(pieces, far, meta, size):
    whole = pl.BlockSpec(memory_space=pltpu.VMEM)
    return pl.pallas_call(
        functools.partial(roll_kernel, size),
        out_shape=[
            jax.ShapeDtypeStruct((2, size, size), bf16),
            jax.ShapeDtypeStruct(far.shape, bf16),
            jax.ShapeDtypeStruct(far.shape, bf16),
        ],
        in_specs=[pl.BlockSpec(memory_space=pltpu.SMEM)] + [whole] * (1 + len(pieces)),
        out_specs=[whole] * 3,
        compiler_params=pltpu.CompilerParams(vmem_limit_bytes=32 * 1024 * 1024),
        cost_estimate=pl.CostEstimate(
            flops=16 * size**3, bytes_accessed=24 * size * size, transcendentals=0
        ),
        name="rolled",
    )(meta, far, *pieces)


def wave_kernel(
    size, span, tile_rows,
    meta, mine, theirs, probe_hbm, far_hbm, far_near_hbm, far_far_hbm, near_hbm, *refs,
):
    measured = refs[:-16]
    keep, send = refs[-16:-14]
    wave, last, probe, amps, far, far_near, far_far, near = refs[-14:-6]
    rows_buf, cols_buf, psi2, zero, sems, amp_sems = refs[-6:]
    offset, live, slot, core = meta[0], meta[1], meta[2], meta[3]
    parts = mine.shape[1]
    half = size // parts

    def chunk(same, other, k):
        return same.at[k // 2] if k % 2 == 0 else other.at[k // 2 + core]

    @pl.when(live == 1)
    def _():
        loads = [
            pltpu.make_async_copy(probe_hbm, probe, sems.at[0]),
            pltpu.make_async_copy(near_hbm, near, sems.at[1]),
            pltpu.make_async_copy(far_near_hbm, far_near, sems.at[2]),
            pltpu.make_async_copy(far_hbm, far, sems.at[3]),
            pltpu.make_async_copy(far_far_hbm, far_far, sems.at[4]),
            pltpu.make_async_copy(chunk(mine, theirs, span), last, sems.at[5]),
        ]
        amp_loads = []
        for number, piece in enumerate(measured):
            rows = piece.shape[0]
            at = pl.multiple_of(jnp.where(slot == number, 0, size - rows), rows)
            amp_loads.append(
                pltpu.make_async_copy(piece, amps.at[pl.ds(at, rows)], amp_sems.at[number])
            )
        chunks = []
        for k in range(span):
            for h in range(parts):
                chunks.append(
                    pltpu.make_async_copy(
                        chunk(mine, theirs, k).at[h],
                        wave.at[:, :, pl.ds(k * tile_rows, tile_rows), pl.ds(h * half, half)],
                        sems.at[6 + parts * k + h],
                    )
                )
        for one in loads[5:] + chunks + loads[:4] + amp_loads + loads[4:5]:
            one.start()
        for one in loads[5:] + chunks:
            one.wait()
        early = lax.broadcasted_iota(jnp.int32, (tile_rows, half), 0) < offset
        for s in range(2):
            for c in range(2):
                for h in range(parts):
                    cols = pl.ds(h * half, half)
                    wave[s, c, 0:tile_rows, cols] = jnp.where(
                        early, last[h, s, c].astype(f32), wave[s, c, 0:tile_rows, cols].astype(f32)
                    ).astype(bf16)

        def put_rows(pair):
            rows_buf[0:size, :] = pair[0].astype(bf16)
            rows_buf[size : 2 * size, :] = pair[1].astype(bf16)

        def put_cols(pair):
            cols_buf[:, 0:size] = pair[0].astype(bf16)
            cols_buf[:, size : 2 * size] = pair[1].astype(bf16)

        def pair_of(ref):
            return ref[0].astype(f32), ref[1].astype(f32)

        loads[0].wait()
        loads[1].wait()
        pr, pi = pair_of(probe)
        ar, ai = pair_of(wave.at[0])
        put_rows((pr * ar - pi * ai, pr * ai + pi * ar))
        put_cols(left(near, False, rows_buf[...], size))
        two = right(near, False, cols_buf[...], size)
        psi2[0] = two[0].astype(bf16)
        psi2[1] = two[1].astype(bf16)
        wr, wi = pair_of(psi2)
        br, bi = pair_of(wave.at[1])
        put_rows((wr * br - wi * bi, wr * bi + wi * br))
        loads[2].wait()
        put_cols(left(far_near, False, rows_buf[...], size))
        loads[3].wait()
        fr, fi = right(far, False, cols_buf[...], size)
        for one in amp_loads:
            one.wait()
        keeping = 1.0 - amps[...].astype(f32) * lax.rsqrt(fr * fr + fi * fi + smooth)
        put_cols((fr * keeping, fi * keeping))
        put_rows(right(far, True, cols_buf[...], size))
        loads[4].wait()
        er, ei = left(far_far, True, rows_buf[...], size)
        br, bi = pair_of(wave.at[1])
        put_cols((br * er + bi * ei, br * ei - bi * er))
        wr, wi = pair_of(psi2)
        wave[1, 0] = (wr * er + wi * ei).astype(bf16)
        wave[1, 1] = (wr * ei - wi * er).astype(bf16)
        put_rows(right(near, True, cols_buf[...], size))
        gr, gi = left(near, True, rows_buf[...], size)
        pr, pi = pair_of(probe)
        wave[0, 0] = (pr * gr + pi * gi).astype(bf16)
        wave[0, 1] = (pr * gi - pi * gr).astype(bf16)
        zero[...] = jnp.zeros(zero.shape, bf16)
        for s in range(2):
            for c in range(2):
                for h in range(parts):
                    cols = pl.ds(h * half, half)
                    both = wave[s, c, 0:tile_rows, cols].astype(f32)
                    last[h, s, c] = jnp.where(early, both, 0.0).astype(bf16)
                    wave[s, c, 0:tile_rows, cols] = jnp.where(early, 0.0, both).astype(bf16)
        stores = [
            pltpu.make_async_copy(last, chunk(keep, send, span), sems.at[5]),
            pltpu.make_async_copy(zero, send.at[(1 - core) * (span // 2)], sems.at[0]),
        ]
        for k in range(span):
            for h in range(parts):
                stores.append(
                    pltpu.make_async_copy(
                        wave.at[:, :, pl.ds(k * tile_rows, tile_rows), pl.ds(h * half, half)],
                        chunk(keep, send, k).at[h],
                        sems.at[6 + parts * k + h],
                    )
                )
        for one in stores:
            one.start()
        for one in stores:
            one.wait()

    @pl.when(live == 0)
    def _():
        zero[...] = jnp.zeros(zero.shape, bf16)
        stores = []
        for k in range(span // 2 + 1):
            stores.append(pltpu.make_async_copy(zero, keep.at[k], sems.at[2 * k]))
            stores.append(pltpu.make_async_copy(zero, send.at[k], sems.at[2 * k + 1]))
        for one in stores:
            one.start()
        for one in stores:
            one.wait()


def waves(mine, theirs, probe_pieces, amp_pieces, meta, size):
    parts, _, _, tile_rows, _ = mine.shape[1:]
    span = size // tile_rows
    far, near = tables(size)
    turned, far_near, far_far = rolled(probe_pieces, far, meta, size)
    anywhere = pl.BlockSpec(memory_space=pl.ANY)
    return pl.pallas_call(
        functools.partial(wave_kernel, size, span, tile_rows),
        out_shape=[jax.ShapeDtypeStruct(mine.shape, bf16)] * 2,
        in_specs=[pl.BlockSpec(memory_space=pltpu.SMEM)] + [anywhere] * (7 + len(amp_pieces)),
        out_specs=[anywhere] * 2,
        scratch_shapes=[
            pltpu.VMEM((2, 2, size, size), bf16),
            pltpu.VMEM(mine.shape[1:], bf16),
            pltpu.VMEM((2, size, size), bf16),
            pltpu.VMEM((size, size), bf16),
            pltpu.VMEM(far.shape, bf16),
            pltpu.VMEM(far.shape, bf16),
            pltpu.VMEM(far.shape, bf16),
            pltpu.VMEM(near.shape, bf16),
            pltpu.VMEM((2 * size, size), bf16),
            pltpu.VMEM((size, 2 * size), bf16),
            pltpu.VMEM((2, size, size), bf16),
            pltpu.VMEM(mine.shape[1:], bf16),
            pltpu.SemaphoreType.DMA((6 + parts * span,)),
            pltpu.SemaphoreType.DMA((len(amp_pieces),)),
        ],
        compiler_params=pltpu.CompilerParams(vmem_limit_bytes=56 * 1024 * 1024),
        cost_estimate=pl.CostEstimate(
            flops=64 * size**3, bytes_accessed=24 * size * size, transcendentals=size * size
        ),
        name="waves",
    )(meta, mine, theirs, turned, far, far_near, far_far, near, *amp_pieces)


def shards(size, object_slab, probe_wave, amplitudes, row_offsets, position_counts):
    tile_rows = object_slab.shape[2]
    span = size // tile_rows
    count = lax.axis_size("tile")
    parts = lax.axis_size("scan")
    slots = amplitudes.shape[0]
    paired = parts == slots == 2
    slot = lax.axis_index("scan")
    ahead = span // 2
    homes = range(ahead, count - ahead)
    swap = [(0, 1), (1, 0)]

    def brought(value, steps):
        return lax.ppermute(value, "tile", [(home + steps, home) for home in homes])

    def returned(value, steps):
        return lax.ppermute(value, "tile", [(home, home + steps) for home in homes])

    def to_partner(value):
        return lax.ppermute(value, "tile", [(home, home ^ 1) for home in homes])

    def by_slot(first, second):
        return jnp.where(slot == 0, first, second)

    own = object_slab.astype(bf16)
    if paired:
        beside = lax.ppermute(own, "scan", swap)
        whole = jnp.stack([by_slot(own, beside), by_slot(beside, own)])
        probe_pieces = [probe_wave, lax.ppermute(probe_wave, "scan", swap)]
    else:
        whole = lax.all_gather(own, "scan")
        every = lax.all_gather(probe_wave, "scan")
        probe_pieces = [every[number] for number in range(parts)]
    notes = brought(jnp.concatenate([row_offsets, position_counts]), -ahead)
    live = (slot < notes[slots]).astype(jnp.int32)
    core = lax.rem(lax.axis_index("tile"), 2)
    meta = jnp.stack(
        [notes[jnp.minimum(slot, slots - 1)], live, slot.astype(jnp.int32), core.astype(jnp.int32)]
    )
    steps = range(-ahead, ahead + 1, 2)
    mine = jnp.stack([brought(whole, step) if step else whole for step in steps])
    theirs = to_partner(mine)
    if paired:
        amp_pieces = [
            lax.ppermute(
                by_slot(amplitudes[which], amplitudes[1 - which]).astype(bf16),
                ("tile", "scan"),
                [
                    ((home - ahead) * 2 + x, home * 2 + (x + which) % 2)
                    for home in homes
                    for x in range(2)
                ],
            )
            for which in range(2)
        ]
    else:
        every = lax.all_gather(brought(amplitudes.astype(bf16), -ahead), "scan")
        amp_pieces = [every[:, jnp.minimum(slot, slots - 1)].reshape((size, size))]
    keep, send = waves(mine, theirs, probe_pieces, amp_pieces, meta, size)
    merged = (keep.astype(f32) + to_partner(send).astype(f32)).astype(bf16)
    total = sum(
        (returned(merged[i], step) if step else merged[i]).astype(f32)
        for i, step in enumerate(steps)
    )
    if paired:
        away = lax.ppermute(by_slot(total[1], total[0]).astype(bf16), "scan", swap)
        return by_slot(total[0], total[1]) + away.astype(f32)
    return lax.psum_scatter(total, "scan", scatter_dimension=0, tiled=False)


def solution(mesh):
    in_specs = (
        P(None, None, "tile", "scan"),
        P(None, None, "scan"),
        P("tile", "scan", None),
        P("tile"),
        P("tile"),
    )
    out_specs = P(None, None, "tile", "scan")

    def run(object_slab, *rest):
        return jax.shard_map(
            functools.partial(shards, object_slab.shape[3]),
            mesh=mesh, in_specs=in_specs, out_specs=out_specs, check_vma=False,
        )(object_slab, *rest)

    return run
```

profile of v0, /device:TPU:16, one launch (start us, length us, event | category | flops | bytes accessed | tf_op | source)
XLA Modules:
  0.0 109.1 jit_solution(9421640509617291745)
XLA Ops:
  1.0 1.6 %collective-permute-start.1 = (bf16[2,2,64,256]{3,2,1,0:T(8,128)(2,1)S(1)}, bf16[2,2,64,256]{3,2,1,0:T(8,128)(2,1)S(1)}, u32[]{:S(2)}, u32[]{:S(2)}) collective-permute-start(bf16[2,2,64,256]{3,2,1,0:T(8,128)(2,1)S(1)} %convert_element_type.52), channel_id=1, source_target_pairs={{0,1},{1,0},{2,3},{3,2},{4,5},{5,4},{6,7},{7,6},{8,9},{9,8},{10,11... | collective-permute-start | bytes 393224 | tf_op jit(solution)/shard_map/ppermute | solution.py:297
  2.5 3.7 %collective-permute-done.1 = bf16[2,2,64,256]{3,2,1,0:T(8,128)(2,1)S(1)} collective-permute-done((bf16[2,2,64,256]{3,2,1,0:T(8,128)(2,1)S(1)}, bf16[2,2,64,256]{3,2,1,0:T(8,128)(2,1)S(1)}, u32[]{:S(2)}, u32[]{:S(2)}) %collective-permute-start.1) | collective-permute-done | bytes 131104 | tf_op jit(solution)/shard_map/ppermute | solution.py:297
  7.3 1.4 %collective-permute-start.2 = (bf16[2,2,2,64,256]{4,3,2,1,0:T(8,128)(2,1)S(1)}, bf16[2,2,2,64,256]{4,3,2,1,0:T(8,128)(2,1)S(1)}, u32[]{:S(2)}, u32[]{:S(2)}) collective-permute-start(bf16[2,2,2,64,256]{4,3,2,1,0:T(8,128)(2,1)S(1)} %pad_maximum_fusion), channel_id=1, source_target_pairs={{0,8},{2,10},{4,12},{6,14},{8,16},{10,18},{12,20},{14,22},{1,9},{3... | collective-permute-start | bytes 786440 | tf_op jit(solution)/shard_map/ppermute | solution.py:284
  8.8 3.4 %collective-permute-start.3 = (bf16[2,2,2,64,256]{4,3,2,1,0:T(8,128)(2,1)S(1)}, bf16[2,2,2,64,256]{4,3,2,1,0:T(8,128)(2,1)S(1)}, u32[]{:S(2)}, u32[]{:S(2)}) collective-permute-start(bf16[2,2,2,64,256]{4,3,2,1,0:T(8,128)(2,1)S(1)} %pad_maximum_fusion), channel_id=1, source_target_pairs={{4,8},{6,10},{8,12},{10,14},{12,16},{14,18},{16,20},{18,22},{5,9},... | collective-permute-start | bytes 786440 | tf_op jit(solution)/shard_map/ppermute | solution.py:284
  12.2 4.0 %collective-permute-start.4 = (bf16[2,2,2,64,256]{4,3,2,1,0:T(8,128)(2,1)S(1)}, bf16[2,2,2,64,256]{4,3,2,1,0:T(8,128)(2,1)S(1)}, u32[]{:S(2)}, u32[]{:S(2)}) collective-permute-start(bf16[2,2,2,64,256]{4,3,2,1,0:T(8,128)(2,1)S(1)} %pad_maximum_fusion), channel_id=1, source_target_pairs={{12,8},{14,10},{16,12},{18,14},{20,16},{22,18},{24,20},{26,22},{13... | collective-permute-start | bytes 786440 | tf_op jit(solution)/shard_map/ppermute | solution.py:284
  16.2 1.9 %collective-permute-start.5 = (bf16[2,2,2,64,256]{4,3,2,1,0:T(8,128)(2,1)S(1)}, bf16[2,2,2,64,256]{4,3,2,1,0:T(8,128)(2,1)S(1)}, u32[]{:S(2)}, u32[]{:S(2)}) collective-permute-start(bf16[2,2,2,64,256]{4,3,2,1,0:T(8,128)(2,1)S(1)} %pad_maximum_fusion), channel_id=1, source_target_pairs={{16,8},{18,10},{20,12},{22,14},{24,16},{26,18},{28,20},{30,22},{17... | collective-permute-start | bytes 786440 | tf_op jit(solution)/shard_map/ppermute | solution.py:284
  18.9 4.3 %collective-permute-done.3 = bf16[2,2,2,64,256]{4,3,2,1,0:T(8,128)(2,1)S(1)} collective-permute-done((bf16[2,2,2,64,256]{4,3,2,1,0:T(8,128)(2,1)S(1)}, bf16[2,2,2,64,256]{4,3,2,1,0:T(8,128)(2,1)S(1)}, u32[]{:S(2)}, u32[]{:S(2)}) %collective-permute-start.3) | collective-permute-done | bytes 262176 | tf_op jit(solution)/shard_map/ppermute | solution.py:284
  24.7 1.9 %collective-permute-done.4 = bf16[2,2,2,64,256]{4,3,2,1,0:T(8,128)(2,1)S(1)} collective-permute-done((bf16[2,2,2,64,256]{4,3,2,1,0:T(8,128)(2,1)S(1)}, bf16[2,2,2,64,256]{4,3,2,1,0:T(8,128)(2,1)S(1)}, u32[]{:S(2)}, u32[]{:S(2)}) %collective-permute-start.4) | collective-permute-done | bytes 262176 | tf_op jit(solution)/shard_map/ppermute | solution.py:284
  28.1 1.9 %collective-permute-start.6 = (bf16[5,2,2,2,64,256]{5,4,3,2,1,0:T(8,128)(2,1)}, bf16[5,2,2,2,64,256]{5,4,3,2,1,0:T(8,128)(2,1)}, u32[]{:S(2)}, u32[]{:S(2)}) collective-permute-start(bf16[5,2,2,2,64,256]{5,4,3,2,1,0:T(8,128)(2,1)} %bitcast_dynamic-update-slice_fusion.mine), channel_id=1, source_target_pairs={{8,10},{10,8},{12,14},{14,12},{16,18},{18,16},{20,22},{22,20},{9,1... | collective-permute-start | bytes 3932168 | tf_op jit(solution)/shard_map/ppermute | solution.py:290
  30.0 1.6 %collective-permute-start.7 = (bf16[2,512,256]{2,1,0:T(8,128)(2,1)S(1)}, bf16[2,512,256]{2,1,0:T(8,128)(2,1)S(1)}, u32[]{:S(2)}, u32[]{:S(2)}) collective-permute-start(bf16[2,512,256]{2,1,0:T(8,128)(2,1)S(1)} %copy-done.1), channel_id=1, source_target_pairs={{0,1},{1,0},{2,3},{3,2},{4,5},{5,4},{6,7},{7,6},{8,9},{9,8},{10,11... | collective-permute-start | bytes 1572872 | tf_op jit(solution)/shard_map/ppermute | solution.py:299
  32.3 1.3 %collective-permute-start = (s32[3]{0:T(128)S(1)}, s32[3]{0:T(128)S(1)}, u32[]{:S(2)}, u32[]{:S(2)}) collective-permute-start(s32[3]{0:T(128)S(1)} %pad_add_fusion), channel_id=1, source_target_pairs={{0,8},{2,10},{4,12},{6,14},{8,16},{10,18},{12,20},{14,22},{1,9},{3... | collective-permute-start | bytes 44 | tf_op jit(solution)/shard_map/ppermute | solution.py:284
  33.7 1.3 %collective-permute-start.9 = (bf16[256,512]{1,0:T(8,128)(2,1)S(1)}, bf16[256,512]{1,0:T(8,128)(2,1)S(1)}, u32[]{:S(2)}, u32[]{:S(2)}) collective-permute-start(bf16[256,512]{1,0:T(8,128)(2,1)S(1)} %get-tuple-element.19), channel_id=1, source_target_pairs={{0,9},{1,8},{2,11},{3,10},{4,13},{5,12},{6,15},{7,14},{8,17},{9,16... | collective-permute-start | bytes 786440 | tf_op jit(solution)/shard_map/ppermute | solution.py:315
  35.0 1.3 %collective-permute-start.8 = (bf16[256,512]{1,0:T(8,128)(2,1)S(1)}, bf16[256,512]{1,0:T(8,128)(2,1)}, u32[]{:S(2)}, u32[]{:S(2)}) collective-permute-start(bf16[256,512]{1,0:T(8,128)(2,1)S(1)} %get-tuple-element.20), channel_id=1, source_target_pairs={{0,8},{1,9},{2,10},{3,11},{4,12},{5,13},{6,14},{7,15},{8,16},{9,17... | collective-permute-start | bytes 786440 | tf_op jit(solution)/shard_map/ppermute | solution.py:315
  36.3 1.4 %collective-permute-done = s32[3]{0:T(128)S(1)} collective-permute-done((s32[3]{0:T(128)S(1)}, s32[3]{0:T(128)S(1)}, u32[]{:S(2)}, u32[]{:S(2)}) %collective-permute-start) | collective-permute-done | bytes 44 | tf_op jit(solution)/shard_map/ppermute | solution.py:284
  39.7 10.3 %collective-permute-done.7.refs_1_ = bf16[2,512,256]{2,1,0:T(8,128)(2,1)S(1)} collective-permute-done((bf16[2,512,256]{2,1,0:T(8,128)(2,1)S(1)}, bf16[2,512,256]{2,1,0:T(8,128)(2,1)S(1)}, u32[]{:S(2)}, u32[]{:S(2)}) %collective-permute-start.7) | collective-permute-done | bytes 524320 | tf_op jit(solution)/shard_map/ppermute | solution.py:299
  50.0 3.0 %rolled.1 = (bf16[2,512,512]{2,1,0:T(8,128)(2,1)S(1)}, bf16[3,512,512]{2,1,0:T(8,128)(2,1)S(1)}, bf16[3,512,512]{2,1,0:T(8,128)(2,1)S(1)}) custom-call(s32[4]{0:T(128)S(1)} %pad_add_fusion.1.meta, bf16[3,512,512]{2,1,0:T(8,128)(2,1)S(1)} %copy-done.2, bf16[2,512,256]{2,1,0:T(8,128)(2,1)S(1)} %copy-done.1, bf16[2,512,256]{2,1,0:T(8,128)(2,1)S(1)} %collective-permute-done.7.refs_1_), custom_call_target="tpu_custom_call" | custom-call | flops 2147483648 | bytes 6291456 | tf_op jit(solution)/shard_map/rolled/pallas_call | solution.py:81
  53.0 1.2 %copy-done.3 = bf16[3,512,512]{2,1,0:T(8,128)(2,1)} copy-done((bf16[3,512,512]{2,1,0:T(8,128)(2,1)}, bf16[3,512,512]{2,1,0:T(8,128)(2,1)S(1)}, u32[]{:S(2)}) %copy-start.3) | copy-done | bytes 1572888
  54.2 1.1 %copy-done.4 = bf16[3,512,512]{2,1,0:T(8,128)(2,1)} copy-done((bf16[3,512,512]{2,1,0:T(8,128)(2,1)}, bf16[3,512,512]{2,1,0:T(8,128)(2,1)S(1)}, u32[]{:S(2)}) %copy-start.4) | copy-done | bytes 1572888
  55.3 1.0 copy-done.5
  57.1 15.7 %waves.1 = (bf16[5,2,2,2,64,256]{5,4,3,2,1,0:T(8,128)(2,1)}, bf16[5,2,2,2,64,256]{5,4,3,2,1,0:T(8,128)(2,1)}) custom-call(s32[4]{0:T(128)} %copy-done, bf16[5,2,2,2,64,256]{5,4,3,2,1,0:T(8,128)(2,1)} %bitcast_dynamic-update-slice_fusion.mine, bf16[5,2,2,2,64,256]{5,4,3,2,1,0:T(8,128)(2,1)} %collective-permute-done.6.theirs, bf16[2,512,512]{2,1,0:T(8,128)(2,1)} %copy-done.5, ...), custom_call_target="tpu_custom_call" | custom-call | flops 8589934592 | bytes 6291456 | tf_op jit(solution)/shard_map/waves/pallas_call | solution.py:242
  72.8 1.9 %collective-permute-start.10 = (bf16[5,2,2,2,64,256]{5,4,3,2,1,0:T(8,128)(2,1)}, bf16[5,2,2,2,64,256]{5,4,3,2,1,0:T(8,128)(2,1)S(1)}, u32[]{:S(2)}, u32[]{:S(2)}) collective-permute-start(bf16[5,2,2,2,64,256]{5,4,3,2,1,0:T(8,128)(2,1)} %get-tuple-element.14), channel_id=1, source_target_pairs={{8,10},{10,8},{12,14},{14,12},{16,18},{18,16},{20,22},{22,20},{9,1... | collective-permute-start | bytes 3932168 | tf_op jit(solution)/shard_map/ppermute | solution.py:290
  74.7 3.2 %collective-permute-done.10 = bf16[5,2,2,2,64,256]{5,4,3,2,1,0:T(8,128)(2,1)S(1)} collective-permute-done((bf16[5,2,2,2,64,256]{5,4,3,2,1,0:T(8,128)(2,1)}, bf16[5,2,2,2,64,256]{5,4,3,2,1,0:T(8,128)(2,1)S(1)}, u32[]{:S(2)}, u32[]{:S(2)}) %collective-permute-start.10) | collective-permute-done | bytes 1310752 | tf_op jit(solution)/shard_map/ppermute | solution.py:290
  77.9 1.8 %add_convert_fusion = bf16[5,2,2,2,64,256]{5,4,3,2,1,0:T(8,128)(2,1)S(1)} fusion(bf16[5,2,2,2,64,256]{5,4,3,2,1,0:T(8,128)(2,1)S(1)} %collective-permute-done.10, bf16[5,2,2,2,64,256]{5,4,3,2,1,0:T(8,128)(2,1)} %get-tuple-element.13), kind=kLoop, calls=%fused_computation | loop fusion | flops 2621440 | bytes 3932160 | tf_op jit(solution)/shard_map/convert_element_type | solution.py:330
  79.8 3.3 %collective-permute-start.11 = (bf16[2,2,2,64,256]{4,3,2,1,0:T(8,128)(2,1)S(1)}, bf16[2,2,2,64,256]{4,3,2,1,0:T(8,128)(2,1)S(1)}, u32[]{:S(2)}, u32[]{:S(2)}) collective-permute-start(bf16[2,2,2,64,256]{4,3,2,1,0:T(8,128)(2,1)S(1)} %get-tuple-element.15), channel_id=1, source_target_pairs={{8,0},{10,2},{12,4},{14,6},{16,8},{18,10},{20,12},{22,14},{9,1},{1... | collective-permute-start | bytes 786440 | tf_op jit(solution)/shard_map/ppermute | solution.py:287
  83.2 1.9 %collective-permute-start.14 = (bf16[2,2,2,64,256]{4,3,2,1,0:T(8,128)(2,1)S(1)}, bf16[2,2,2,64,256]{4,3,2,1,0:T(8,128)(2,1)S(1)}, u32[]{:S(2)}, u32[]{:S(2)}) collective-permute-start(bf16[2,2,2,64,256]{4,3,2,1,0:T(8,128)(2,1)S(1)} %get-tuple-element.16), channel_id=1, source_target_pairs={{8,16},{10,18},{12,20},{14,22},{16,24},{18,26},{20,28},{22,30},{9,... | collective-permute-start | bytes 786440 | tf_op jit(solution)/shard_map/ppermute | solution.py:287
  85.1 2.7 %collective-permute-start.13 = (bf16[2,2,2,64,256]{4,3,2,1,0:T(8,128)(2,1)S(1)}, bf16[2,2,2,64,256]{4,3,2,1,0:T(8,128)(2,1)S(1)}, u32[]{:S(2)}, u32[]{:S(2)}) collective-permute-start(bf16[2,2,2,64,256]{4,3,2,1,0:T(8,128)(2,1)S(1)} %get-tuple-element.17), channel_id=1, source_target_pairs={{8,12},{10,14},{12,16},{14,18},{16,20},{18,22},{20,24},{22,26},{9,... | collective-permute-start | bytes 786440 | tf_op jit(solution)/shard_map/ppermute | solution.py:287
  87.8 4.1 %collective-permute-start.12 = (bf16[2,2,2,64,256]{4,3,2,1,0:T(8,128)(2,1)S(1)}, bf16[2,2,2,64,256]{4,3,2,1,0:T(8,128)(2,1)S(1)}, u32[]{:S(2)}, u32[]{:S(2)}) collective-permute-start(bf16[2,2,2,64,256]{4,3,2,1,0:T(8,128)(2,1)S(1)} %get-tuple-element.18), channel_id=1, source_target_pairs={{8,4},{10,6},{12,8},{14,10},{16,12},{18,14},{20,16},{22,18},{9,5},... | collective-permute-start | bytes 786440 | tf_op jit(solution)/shard_map/ppermute | solution.py:287
  91.9 1.3 %collective-permute-done.14 = bf16[2,2,2,64,256]{4,3,2,1,0:T(8,128)(2,1)S(1)} collective-permute-done((bf16[2,2,2,64,256]{4,3,2,1,0:T(8,128)(2,1)S(1)}, bf16[2,2,2,64,256]{4,3,2,1,0:T(8,128)(2,1)S(1)}, u32[]{:S(2)}, u32[]{:S(2)}) %collective-permute-start.14) | collective-permute-done | bytes 262176 | tf_op jit(solution)/shard_map/ppermute | solution.py:287
  93.1 5.9 %collective-permute-done.13 = bf16[2,2,2,64,256]{4,3,2,1,0:T(8,128)(2,1)S(1)} collective-permute-done((bf16[2,2,2,64,256]{4,3,2,1,0:T(8,128)(2,1)S(1)}, bf16[2,2,2,64,256]{4,3,2,1,0:T(8,128)(2,1)S(1)}, u32[]{:S(2)}, u32[]{:S(2)}) %collective-permute-start.13) | collective-permute-done | bytes 262176 | tf_op jit(solution)/shard_map/ppermute | solution.py:287
  99.0 4.0 %collective-permute-done.12 = bf16[2,2,2,64,256]{4,3,2,1,0:T(8,128)(2,1)S(1)} collective-permute-done((bf16[2,2,2,64,256]{4,3,2,1,0:T(8,128)(2,1)S(1)}, bf16[2,2,2,64,256]{4,3,2,1,0:T(8,128)(2,1)S(1)}, u32[]{:S(2)}, u32[]{:S(2)}) %collective-permute-start.12) | collective-permute-done | bytes 262176 | tf_op jit(solution)/shard_map/ppermute | solution.py:287
  103.3 1.6 %collective-permute-start.15 = (bf16[2,2,64,256]{3,2,1,0:T(8,128)(2,1)S(1)}, bf16[2,2,64,256]{3,2,1,0:T(8,128)(2,1)S(1)}, u32[]{:S(2)}, u32[]{:S(2)}) collective-permute-start(bf16[2,2,64,256]{3,2,1,0:T(8,128)(2,1)S(1)} %fusion.4), channel_id=1, source_target_pairs={{0,1},{1,0},{2,3},{3,2},{4,5},{5,4},{6,7},{7,6},{8,9},{9,8},{10,11... | collective-permute-start | bytes 393224 | tf_op jit(solution)/shard_map/ppermute | solution.py:336
  104.8 3.5 %collective-permute-done.15 = bf16[2,2,64,256]{3,2,1,0:T(8,128)(2,1)S(1)} collective-permute-done((bf16[2,2,64,256]{3,2,1,0:T(8,128)(2,1)S(1)}, bf16[2,2,64,256]{3,2,1,0:T(8,128)(2,1)S(1)}, u32[]{:S(2)}, u32[]{:S(2)}) %collective-permute-start.15) | collective-permute-done | bytes 131104 | tf_op jit(solution)/shard_map/ppermute | solution.py:336
  (37 shorter events, 8.9 us)
Async XLA Ops:
  1.0 5.3 %collective-permute-start.1 = (bf16[2,2,64,256]{3,2,1,0:T(8,128)(2,1)S(1)}, bf16[2,2,64,256]{3,2,1,0:T(8,128)(2,1)S(1)}, u32[]{:S(2)}, u32[]{:S(2)}) collective-permute-start(bf16[2,2,64,256]{3,2,1,0:T(8,128)(2,1)S(1)} %convert_element_type.52), channel_id=1, source_target_pairs={{0,1},{1,0},{2,3},{3,2},{4,5},{5,4},{6,7},{7,6},{8,9},{9,8},{10,11... | collective-permute-start | bytes 393224 | tf_op jit(solution)/shard_map/ppermute | solution.py:297
  7.3 22.7 %copy-start.1 = (bf16[2,512,256]{2,1,0:T(8,128)(2,1)S(1)}, bf16[2,512,256]{2,1,0:T(8,128)(2,1)}, u32[]{:S(2)}) copy-start(bf16[2,512,256]{2,1,0:T(8,128)(2,1)} %refs_0_.1) | copy-start | bytes 1572868
  7.3 24.9 %copy-start.8 = (s32[2]{0:T(128)S(1)}, s32[2]{0:T(128)}, u32[]{:S(2)}) copy-start(s32[2]{0:T(128)} %param.10) | copy-start | bytes 28
  7.3 26.3 %copy-start.6 = (f32[2,256,512]{2,1,0:T(8,128)S(1)}, f32[2,256,512]{2,1,0:T(8,128)}, u32[]{:S(2)}) copy-start(f32[2,256,512]{2,1,0:T(8,128)} %param.9) | copy-start | bytes 3145732
  7.3 10.8 %collective-permute-start.2 = (bf16[2,2,2,64,256]{4,3,2,1,0:T(8,128)(2,1)S(1)}, bf16[2,2,2,64,256]{4,3,2,1,0:T(8,128)(2,1)S(1)}, u32[]{:S(2)}, u32[]{:S(2)}) collective-permute-start(bf16[2,2,2,64,256]{4,3,2,1,0:T(8,128)(2,1)S(1)} %pad_maximum_fusion), channel_id=1, source_target_pairs={{0,8},{2,10},{4,12},{6,14},{8,16},{10,18},{12,20},{14,22},{1,9},{3... | collective-permute-start | bytes 786440 | tf_op jit(solution)/shard_map/ppermute | solution.py:284
  8.8 14.5 %collective-permute-start.3 = (bf16[2,2,2,64,256]{4,3,2,1,0:T(8,128)(2,1)S(1)}, bf16[2,2,2,64,256]{4,3,2,1,0:T(8,128)(2,1)S(1)}, u32[]{:S(2)}, u32[]{:S(2)}) collective-permute-start(bf16[2,2,2,64,256]{4,3,2,1,0:T(8,128)(2,1)S(1)} %pad_maximum_fusion), channel_id=1, source_target_pairs={{4,8},{6,10},{8,12},{10,14},{12,16},{14,18},{16,20},{18,22},{5,9},... | collective-permute-start | bytes 786440 | tf_op jit(solution)/shard_map/ppermute | solution.py:284
  12.2 14.4 %collective-permute-start.4 = (bf16[2,2,2,64,256]{4,3,2,1,0:T(8,128)(2,1)S(1)}, bf16[2,2,2,64,256]{4,3,2,1,0:T(8,128)(2,1)S(1)}, u32[]{:S(2)}, u32[]{:S(2)}) collective-permute-start(bf16[2,2,2,64,256]{4,3,2,1,0:T(8,128)(2,1)S(1)} %pad_maximum_fusion), channel_id=1, source_target_pairs={{12,8},{14,10},{16,12},{18,14},{20,16},{22,18},{24,20},{26,22},{13... | collective-permute-start | bytes 786440 | tf_op jit(solution)/shard_map/ppermute | solution.py:284
  16.2 11.1 %collective-permute-start.5 = (bf16[2,2,2,64,256]{4,3,2,1,0:T(8,128)(2,1)S(1)}, bf16[2,2,2,64,256]{4,3,2,1,0:T(8,128)(2,1)S(1)}, u32[]{:S(2)}, u32[]{:S(2)}) collective-permute-start(bf16[2,2,2,64,256]{4,3,2,1,0:T(8,128)(2,1)S(1)} %pad_maximum_fusion), channel_id=1, source_target_pairs={{16,8},{18,10},{20,12},{22,14},{24,16},{26,18},{28,20},{30,22},{17... | collective-permute-start | bytes 786440 | tf_op jit(solution)/shard_map/ppermute | solution.py:284
  23.9 26.1 %copy-start.2 = (bf16[3,512,512]{2,1,0:T(8,128)(2,1)S(1)}, bf16[3,512,512]{2,1,0:T(8,128)(2,1)}, u32[]{:S(2)}) copy-start(bf16[3,512,512]{2,1,0:T(8,128)(2,1)} %constant.21.clone.far.far_hbm) | copy-start | bytes 4718596
  28.1 28.3 %collective-permute-start.6 = (bf16[5,2,2,2,64,256]{5,4,3,2,1,0:T(8,128)(2,1)}, bf16[5,2,2,2,64,256]{5,4,3,2,1,0:T(8,128)(2,1)}, u32[]{:S(2)}, u32[]{:S(2)}) collective-permute-start(bf16[5,2,2,2,64,256]{5,4,3,2,1,0:T(8,128)(2,1)} %bitcast_dynamic-update-slice_fusion.mine), channel_id=1, source_target_pairs={{8,10},{10,8},{12,14},{14,12},{16,18},{18,16},{20,22},{22,20},{9,1... | collective-permute-start | bytes 3932168 | tf_op jit(solution)/shard_map/ppermute | solution.py:290
  30.0 20.0 %collective-permute-start.7 = (bf16[2,512,256]{2,1,0:T(8,128)(2,1)S(1)}, bf16[2,512,256]{2,1,0:T(8,128)(2,1)S(1)}, u32[]{:S(2)}, u32[]{:S(2)}) collective-permute-start(bf16[2,512,256]{2,1,0:T(8,128)(2,1)S(1)} %copy-done.1), channel_id=1, source_target_pairs={{0,1},{1,0},{2,3},{3,2},{4,5},{5,4},{6,7},{7,6},{8,9},{9,8},{10,11... | collective-permute-start | bytes 1572872 | tf_op jit(solution)/shard_map/ppermute | solution.py:299
  32.3 5.4 %collective-permute-start = (s32[3]{0:T(128)S(1)}, s32[3]{0:T(128)S(1)}, u32[]{:S(2)}, u32[]{:S(2)}) collective-permute-start(s32[3]{0:T(128)S(1)} %pad_add_fusion), channel_id=1, source_target_pairs={{0,8},{2,10},{4,12},{6,14},{8,16},{10,18},{12,20},{14,22},{1,9},{3... | collective-permute-start | bytes 44 | tf_op jit(solution)/shard_map/ppermute | solution.py:284
  33.7 22.7 %collective-permute-start.9 = (bf16[256,512]{1,0:T(8,128)(2,1)S(1)}, bf16[256,512]{1,0:T(8,128)(2,1)S(1)}, u32[]{:S(2)}, u32[]{:S(2)}) collective-permute-start(bf16[256,512]{1,0:T(8,128)(2,1)S(1)} %get-tuple-element.19), channel_id=1, source_target_pairs={{0,9},{1,8},{2,11},{3,10},{4,13},{5,12},{6,15},{7,14},{8,17},{9,16... | collective-permute-start | bytes 786440 | tf_op jit(solution)/shard_map/ppermute | solution.py:315
  35.0 21.4 %collective-permute-start.8 = (bf16[256,512]{1,0:T(8,128)(2,1)S(1)}, bf16[256,512]{1,0:T(8,128)(2,1)}, u32[]{:S(2)}, u32[]{:S(2)}) collective-permute-start(bf16[256,512]{1,0:T(8,128)(2,1)S(1)} %get-tuple-element.20), channel_id=1, source_target_pairs={{0,8},{1,9},{2,10},{3,11},{4,12},{5,13},{6,14},{7,15},{8,16},{9,17... | collective-permute-start | bytes 786440 | tf_op jit(solution)/shard_map/ppermute | solution.py:315
  39.7 13.3 %copy-start = (s32[4]{0:T(128)}, s32[4]{0:T(128)S(1)}, u32[]{:S(2)}) copy-start(s32[4]{0:T(128)S(1)} %pad_add_fusion.1.meta) | copy-start | bytes 52
  53.0 1.2 %copy-start.3 = (bf16[3,512,512]{2,1,0:T(8,128)(2,1)}, bf16[3,512,512]{2,1,0:T(8,128)(2,1)S(1)}, u32[]{:S(2)}) copy-start(bf16[3,512,512]{2,1,0:T(8,128)(2,1)S(1)} %get-tuple-element.11.far_near_hbm) | copy-start | bytes 4718596
  54.2 1.1 %copy-start.4 = (bf16[3,512,512]{2,1,0:T(8,128)(2,1)}, bf16[3,512,512]{2,1,0:T(8,128)(2,1)S(1)}, u32[]{:S(2)}) copy-start(bf16[3,512,512]{2,1,0:T(8,128)(2,1)S(1)} %get-tuple-element.12.far_far_hbm) | copy-start | bytes 4718596
  55.3 1.0 copy-start.5
  56.4 0.7 copy-start.7
  72.8 5.1 %collective-permute-start.10 = (bf16[5,2,2,2,64,256]{5,4,3,2,1,0:T(8,128)(2,1)}, bf16[5,2,2,2,64,256]{5,4,3,2,1,0:T(8,128)(2,1)S(1)}, u32[]{:S(2)}, u32[]{:S(2)}) collective-permute-start(bf16[5,2,2,2,64,256]{5,4,3,2,1,0:T(8,128)(2,1)} %get-tuple-element.14), channel_id=1, source_target_pairs={{8,10},{10,8},{12,14},{14,12},{16,18},{18,16},{20,22},{22,20},{9,1... | collective-permute-start | bytes 3932168 | tf_op jit(solution)/shard_map/ppermute | solution.py:290
  79.8 12.0 %collective-permute-start.11 = (bf16[2,2,2,64,256]{4,3,2,1,0:T(8,128)(2,1)S(1)}, bf16[2,2,2,64,256]{4,3,2,1,0:T(8,128)(2,1)S(1)}, u32[]{:S(2)}, u32[]{:S(2)}) collective-permute-start(bf16[2,2,2,64,256]{4,3,2,1,0:T(8,128)(2,1)S(1)} %get-tuple-element.15), channel_id=1, source_target_pairs={{8,0},{10,2},{12,4},{14,6},{16,8},{18,10},{20,12},{22,14},{9,1},{1... | collective-permute-start | bytes 786440 | tf_op jit(solution)/shard_map/ppermute | solution.py:287
  83.2 10.0 %collective-permute-start.14 = (bf16[2,2,2,64,256]{4,3,2,1,0:T(8,128)(2,1)S(1)}, bf16[2,2,2,64,256]{4,3,2,1,0:T(8,128)(2,1)S(1)}, u32[]{:S(2)}, u32[]{:S(2)}) collective-permute-start(bf16[2,2,2,64,256]{4,3,2,1,0:T(8,128)(2,1)S(1)} %get-tuple-element.16), channel_id=1, source_target_pairs={{8,16},{10,18},{12,20},{14,22},{16,24},{18,26},{20,28},{22,30},{9,... | collective-permute-start | bytes 786440 | tf_op jit(solution)/shard_map/ppermute | solution.py:287
  85.1 14.0 %collective-permute-start.13 = (bf16[2,2,2,64,256]{4,3,2,1,0:T(8,128)(2,1)S(1)}, bf16[2,2,2,64,256]{4,3,2,1,0:T(8,128)(2,1)S(1)}, u32[]{:S(2)}, u32[]{:S(2)}) collective-permute-start(bf16[2,2,2,64,256]{4,3,2,1,0:T(8,128)(2,1)S(1)} %get-tuple-element.17), channel_id=1, source_target_pairs={{8,12},{10,14},{12,16},{14,18},{16,20},{18,22},{20,24},{22,26},{9,... | collective-permute-start | bytes 786440 | tf_op jit(solution)/shard_map/ppermute | solution.py:287
  87.8 15.3 %collective-permute-start.12 = (bf16[2,2,2,64,256]{4,3,2,1,0:T(8,128)(2,1)S(1)}, bf16[2,2,2,64,256]{4,3,2,1,0:T(8,128)(2,1)S(1)}, u32[]{:S(2)}, u32[]{:S(2)}) collective-permute-start(bf16[2,2,2,64,256]{4,3,2,1,0:T(8,128)(2,1)S(1)} %get-tuple-element.18), channel_id=1, source_target_pairs={{8,4},{10,6},{12,8},{14,10},{16,12},{18,14},{20,16},{22,18},{9,5},... | collective-permute-start | bytes 786440 | tf_op jit(solution)/shard_map/ppermute | solution.py:287
  103.3 5.0 %collective-permute-start.15 = (bf16[2,2,64,256]{3,2,1,0:T(8,128)(2,1)S(1)}, bf16[2,2,64,256]{3,2,1,0:T(8,128)(2,1)S(1)}, u32[]{:S(2)}, u32[]{:S(2)}) collective-permute-start(bf16[2,2,64,256]{3,2,1,0:T(8,128)(2,1)S(1)} %fusion.4), channel_id=1, source_target_pairs={{0,1},{1,0},{2,3},{3,2},{4,5},{5,4},{6,7},{7,6},{8,9},{9,8},{10,11... | collective-permute-start | bytes 393224 | tf_op jit(solution)/shard_map/ppermute | solution.py:336
where the time goes:
time: 110 us; the launch traced here: 109 us
  waiting for transfers between devices  39.7 us (36%)
  starting transfers between devices  35.1 us (32%)
  Pallas kernels  18.7 us (17%)
  local copies, waits for them, and re-layouts  7.72 us (7%)
  other arithmetic  6.3 us (6%)
  between operations  1.57 us (1%)
    pallas_call x1, Pallas kernels, waves(): pl.pallas_call(functools.partial(wave_kernel, size, span, tile_rows), out...  15.7 us
    ppermute x5, starting transfers between devices, brought(): return lax.ppermute(value, 'tile', [(home + steps, home) for home in homes])  12.1 us
    ppermute x4, starting transfers between devices, returned(): return lax.ppermute(value, 'tile', [(home, home + steps) for home in homes])  12 us
    ppermute x4, waiting for transfers between devices, returned(): return lax.ppermute(value, 'tile', [(home, home + steps) for home in homes])  11.2 us
    ppermute x1, waiting for transfers between devices, shards(): probe_pieces = [probe_wave, lax.ppermute(probe_wave, 'scan', swap)]  10.3 us
    ppermute x5, waiting for transfers between devices, brought(): return lax.ppermute(value, 'tile', [(home + steps, home) for home in homes])  7.73 us
    unnamed x21, local copies, waits for them, and re-layouts  6.27 us
    ppermute x2, starting transfers between devices, to_partner(): return lax.ppermute(value, 'tile', [(home, home ^ 1) for home in homes])  3.83 us
  transfers between devices with their start and end apart: 16, of which 10 were waited for; matrix products, arithmetic and copies ran while one was open for 4% of the time, Pallas kernels for 3%

commit v1 on v0

v1 whole, which is shorter than its diff:
```python
import functools
import math

import jax
import jax.numpy as jnp
import ml_dtypes
import numpy as np
from jax import lax
from jax.experimental import pallas as pl
from jax.experimental.pallas import tpu as pltpu
from jax.sharding import PartitionSpec as P

fresnel = 0.5
smooth = 1.0
bf16 = jnp.bfloat16
f32 = jnp.float32


def tables(size):
    index = np.arange(size)
    angles = 2.0 * np.pi / size * (index[:, None] * index[None, :] % size)
    base = np.exp(1j * angles)
    far = np.conj(base) / math.sqrt(size)
    centred = np.where(index < size // 2, index, index - size).astype(np.float64)
    kernel = np.exp(-1j * np.pi * fresnel / size * centred * centred)
    near = (base * kernel[None, :]) @ np.conj(base).T / size

    def parts(table):
        stacked = np.stack([table.real, table.imag, -table.imag])
        return jnp.asarray(stacked.astype(ml_dtypes.bfloat16))

    order = np.concatenate([index[0::2], index[1::2]])
    return parts(far[order]), parts(far[:, order]), parts(near)


def left(table, conjugate, wave):
    real, plus, minus = table if not conjugate else (table[0], table[2], table[1])
    top = jnp.concatenate([real, minus], axis=1)
    bottom = jnp.concatenate([plus, real], axis=1)
    return (
        jnp.dot(top, wave, preferred_element_type=f32),
        jnp.dot(bottom, wave, preferred_element_type=f32),
    )


def right(table, conjugate, wave):
    real, plus, minus = table if not conjugate else (table[0], table[2], table[1])
    real_side = jnp.concatenate([real, minus], axis=0)
    imag_side = jnp.concatenate([plus, real], axis=0)
    return (
        jnp.dot(wave, real_side, preferred_element_type=f32),
        jnp.dot(wave, imag_side, preferred_element_type=f32),
    )


def one_hot(size, hit):
    row = lax.broadcasted_iota(jnp.int32, (size, size), 0)
    col = lax.broadcasted_iota(jnp.int32, (size, size), 1)
    return jnp.where(hit(row, col), 1.0, 0.0).astype(bf16)


def roll_kernel(size, count, meta, far_rows, far_cols, *refs):
    pieces, measured = refs[:count], refs[count:-5]
    probe_out, near_side, far_side, ordered, amps = refs[-5:]
    offset, slot = meta[0], meta[2]
    half = size // 2

    def moved(to, source):
        gap = to - source - offset
        return (gap == 0) | (gap == -size)

    down = one_hot(size, moved)
    across = one_hot(size, lambda row, col: moved(col, row))
    for c in range(3):
        near_side[c] = jnp.dot(
            far_rows[c], across[:, :half], preferred_element_type=f32
        ).astype(bf16)
        far_side[c] = jnp.dot(down[:half], far_cols[c], preferred_element_type=f32).astype(bf16)
    for c in range(2):
        done = 0
        for piece in pieces:
            turned = jnp.dot(down, piece[c], preferred_element_type=f32).astype(bf16)
            width = turned.shape[1]
            if len(pieces) == 2:
                at = pl.multiple_of(jnp.where(slot == done, 0, width), width)
                probe_out[c, :, pl.ds(at, width)] = turned
                done += 1
            else:
                probe_out[c, :, done : done + width] = turned
                done += width
    for number, piece in enumerate(measured):
        rows = piece.shape[0]
        at = pl.multiple_of(jnp.where(slot == number, 0, size - rows), rows)
        amps[pl.ds(at, rows), :] = piece[...]

    def frequency(place, natural):
        return natural == jnp.where(place < half, 2 * place, 2 * (place - half) + 1)

    rows_first = jnp.dot(one_hot(size, frequency), amps[...], preferred_element_type=f32)
    ordered[...] = jnp.dot(
        rows_first.astype(bf16),
        one_hot(size, lambda row, col: frequency(col, row)),
        preferred_element_type=f32,
    ).astype(bf16)


def rolled(pieces, amp_pieces, far_rows, far_cols, meta, size):
    whole = pl.BlockSpec(memory_space=pltpu.VMEM)
    return pl.pallas_call(
        functools.partial(roll_kernel, size, len(pieces)),
        out_shape=[
            jax.ShapeDtypeStruct((2, size, size), bf16),
            jax.ShapeDtypeStruct((3, size, size // 2), bf16),
            jax.ShapeDtypeStruct((3, size // 2, size), bf16),
            jax.ShapeDtypeStruct((size, size), bf16),
        ],
        in_specs=[pl.BlockSpec(memory_space=pltpu.SMEM)]
        + [whole] * (2 + len(pieces) + len(amp_pieces)),
        out_specs=[whole] * 4,
        scratch_shapes=[pltpu.VMEM((size, size), bf16)],
        compiler_params=pltpu.CompilerParams(vmem_limit_bytes=24 * 1024 * 1024),
        cost_estimate=pl.CostEstimate(
            flops=64 * size**3, bytes_accessed=24 * size * size, transcendentals=0
        ),
        name="rolled",
    )(meta, far_rows, far_cols, *pieces, *amp_pieces)


def wave_kernel(
    size, span, tile_rows,
    meta, mine, theirs, far_rows_hbm, far_cols_hbm, near_hbm, probe, far_near, far_far, amps,
    keep, send, wave, last, far_rows, far_cols, near, rows_buf, cols_buf, psi2, zero, sems,
):
    offset, live, core = meta[0], meta[1], meta[3]
    parts = mine.shape[1]
    width = size // parts
    half = size // 2
    low, high = slice(0, half), slice(half, size)

    def chunk(same, other, k):
        return same.at[k // 2] if k % 2 == 0 else other.at[k // 2 + core]

    @pl.when(live == 1)
    def _():
        loads = [
            pltpu.make_async_copy(chunk(mine, theirs, span), last, sems.at[0]),
            pltpu.make_async_copy(near_hbm, near, sems.at[1]),
            pltpu.make_async_copy(far_cols_hbm.at[:, pl.ds(0, half)], far_cols, sems.at[2]),
            pltpu.make_async_copy(far_rows_hbm.at[:, :, pl.ds(0, half)], far_rows, sems.at[3]),
        ]
        chunks = []
        for k in range(span):
            for h in range(parts):
                chunks.append(
                    pltpu.make_async_copy(
                        chunk(mine, theirs, k).at[h],
                        wave.at[:, :, pl.ds(k * tile_rows, tile_rows), pl.ds(h * width, width)],
                        sems.at[4 + parts * k + h],
                    )
                )
        for one in loads[:1] + chunks + loads[1:]:
            one.start()
        for one in loads[:1] + chunks:
            one.wait()
        early = lax.broadcasted_iota(jnp.int32, (tile_rows, width), 0) < offset
        for s in range(2):
            for c in range(2):
                for h in range(parts):
                    cols = pl.ds(h * width, width)
                    wave[s, c, 0:tile_rows, cols] = jnp.where(
                        early, last[h, s, c].astype(f32), wave[s, c, 0:tile_rows, cols].astype(f32)
                    ).astype(bf16)

        def put_rows(pair):
            rows_buf[0:size, :] = pair[0].astype(bf16)
            rows_buf[size : 2 * size, :] = pair[1].astype(bf16)

        def put_cols(pair):
            cols_buf[:, 0:size] = pair[0].astype(bf16)
            cols_buf[:, size : 2 * size] = pair[1].astype(bf16)

        def pair_of(ref):
            return ref[0].astype(f32), ref[1].astype(f32)

        def parts_of(ref, rows, cols):
            return ref[0, rows, cols], ref[1, rows, cols], ref[2, rows, cols]

        def put_row_halves(first, second):
            for number, wave_half in enumerate((first, second)):
                for c in range(2):
                    at = number * size + c * half
                    rows_buf[at : at + half, :] = wave_half[c].astype(bf16)

        def put_col_halves(first, second):
            for number, wave_half in enumerate((first, second)):
                for c in range(2):
                    at = number * size + c * half
                    cols_buf[:, at : at + half] = wave_half[c].astype(bf16)

        def both(first, second, axis):
            return [jnp.concatenate([a, b], axis=axis) for a, b in zip(first, second)]

        def plus(first, second):
            return [a + b for a, b in zip(first, second)]

        def less(first, second):
            return [a - b for a, b in zip(first, second)]

        everything = slice(None)
        loads[1].wait()
        near_parts = parts_of(near, everything, everything)
        pr, pi = pair_of(probe)
        ar, ai = pair_of(wave.at[0])
        put_rows((pr * ar - pi * ai, pr * ai + pi * ar))
        put_cols(left(near_parts, False, rows_buf[...]))
        two = right(near_parts, False, cols_buf[...])
        psi2[0] = two[0].astype(bf16)
        psi2[1] = two[1].astype(bf16)
        wr, wi = pair_of(psi2)
        br, bi = pair_of(wave.at[1])
        wave_exit = (wr * br - wi * bi, wr * bi + wi * br)
        top, bottom = [x[low] for x in wave_exit], [x[high] for x in wave_exit]
        put_row_halves(plus(top, bottom), less(top, bottom))
        half2 = both(
            left(parts_of(far_near, low, everything), False, rows_buf[0:size, :]),
            left(parts_of(far_near, high, everything), False, rows_buf[size : 2 * size, :]),
            0,
        )
        top, bottom = [x[:, low] for x in half2], [x[:, high] for x in half2]
        put_col_halves(plus(top, bottom), less(top, bottom))
        loads[2].wait()
        fields = [
            right(parts_of(far_cols, everything, low), False, cols_buf[:, 0:size]),
            right(parts_of(far_cols, everything, high), False, cols_buf[:, size : 2 * size]),
        ]
        chis = []
        for (fr, fi), cols in zip(fields, (low, high)):
            keeping = 1.0 - amps[:, cols].astype(f32) * lax.rsqrt(fr * fr + fi * fi + smooth)
            chis.append((fr * keeping, fi * keeping))
        put_col_halves(*chis)
        loads[3].wait()
        even = right(parts_of(far_rows, low, everything), True, cols_buf[:, 0:size])
        odd = right(parts_of(far_rows, high, everything), True, cols_buf[:, size : 2 * size])
        back1 = both(plus(even, odd), less(even, odd), 1)
        put_row_halves([x[low] for x in back1], [x[high] for x in back1])
        even = left(parts_of(far_far, everything, low), True, rows_buf[0:size, :])
        odd = left(parts_of(far_far, everything, high), True, rows_buf[size : 2 * size, :])
        er, ei = both(plus(even, odd), less(even, odd), 0)
        br, bi = pair_of(wave.at[1])
        put_cols((br * er + bi * ei, br * ei - bi * er))
        wr, wi = pair_of(psi2)
        wave[1, 0] = (wr * er + wi * ei).astype(bf16)
        wave[1, 1] = (wr * ei - wi * er).astype(bf16)
        near_parts = parts_of(near, everything, everything)
        put_rows(right(near_parts, True, cols_buf[...]))
        gr, gi = left(near_parts, True, rows_buf[...])
        pr, pi = pair_of(probe)
        wave[0, 0] = (pr * gr + pi * gi).astype(bf16)
        wave[0, 1] = (pr * gi - pi * gr).astype(bf16)
        zero[...] = jnp.zeros(zero.shape, bf16)
        for s in range(2):
            for c in range(2):
                for h in range(parts):
                    cols = pl.ds(h * width, width)
                    mixed = wave[s, c, 0:tile_rows, cols].astype(f32)
                    last[h, s, c] = jnp.where(early, mixed, 0.0).astype(bf16)
                    wave[s, c, 0:tile_rows, cols] = jnp.where(early, 0.0, mixed).astype(bf16)
        stores = [
            pltpu.make_async_copy(last, chunk(keep, send, span), sems.at[0]),
            pltpu.make_async_copy(zero, send.at[(1 - core) * (span // 2)], sems.at[1]),
        ]
        for k in range(span):
            for h in range(parts):
                stores.append(
                    pltpu.make_async_copy(
                        wave.at[:, :, pl.ds(k * tile_rows, tile_rows), pl.ds(h * width, width)],
                        chunk(keep, send, k).at[h],
                        sems.at[4 + parts * k + h],
                    )
                )
        for one in stores:
            one.start()
        for one in stores:
            one.wait()

    @pl.when(live == 0)
    def _():
        zero[...] = jnp.zeros(zero.shape, bf16)
        stores = []
        for k in range(span // 2 + 1):
            stores.append(pltpu.make_async_copy(zero, keep.at[k], sems.at[2 * k]))
            stores.append(pltpu.make_async_copy(zero, send.at[k], sems.at[2 * k + 1]))
        for one in stores:
            one.start()
        for one in stores:
            one.wait()


def waves(mine, theirs, consts, turned, meta, size):
    parts, _, _, tile_rows, _ = mine.shape[1:]
    span = size // tile_rows
    anywhere = pl.BlockSpec(memory_space=pl.ANY)
    inside = pl.BlockSpec(memory_space=pltpu.VMEM)
    return pl.pallas_call(
        functools.partial(wave_kernel, size, span, tile_rows),
        out_shape=[jax.ShapeDtypeStruct(mine.shape, bf16)] * 2,
        in_specs=[pl.BlockSpec(memory_space=pltpu.SMEM)]
        + [anywhere] * 5
        + [inside] * 4,
        out_specs=[anywhere] * 2,
        scratch_shapes=[
            pltpu.VMEM((2, 2, size, size), bf16),
            pltpu.VMEM(mine.shape[1:], bf16),
            pltpu.VMEM((3, size, size // 2), bf16),
            pltpu.VMEM((3, size // 2, size), bf16),
            pltpu.VMEM((3, size, size), bf16),
            pltpu.VMEM((2 * size, size), bf16),
            pltpu.VMEM((size, 2 * size), bf16),
            pltpu.VMEM((2, size, size), bf16),
            pltpu.VMEM(mine.shape[1:], bf16),
            pltpu.SemaphoreType.DMA((4 + parts * span,)),
        ],
        compiler_params=pltpu.CompilerParams(vmem_limit_bytes=48 * 1024 * 1024),
        cost_estimate=pl.CostEstimate(
            flops=64 * size**3, bytes_accessed=24 * size * size, transcendentals=size * size
        ),
        name="waves",
    )(meta, mine, theirs, *consts, *turned)


def shards(size, object_slab, probe_wave, amplitudes, row_offsets, position_counts):
    tile_rows = object_slab.shape[2]
    span = size // tile_rows
    count = lax.axis_size("tile")
    parts = lax.axis_size("scan")
    slots = amplitudes.shape[0]
    paired = parts == slots == 2
    slot = lax.axis_index("scan")
    ahead = span // 2
    homes = range(ahead, count - ahead)
    swap = [(0, 1), (1, 0)]

    def brought(value, steps):
        return lax.ppermute(value, "tile", [(home + steps, home) for home in homes])

    def returned(value, steps):
        return lax.ppermute(value, "tile", [(home, home + steps) for home in homes])

    def to_partner(value):
        return lax.ppermute(value, "tile", [(home, home ^ 1) for home in homes])

    def by_slot(first, second):
        return jnp.where(slot == 0, first, second)

    own = object_slab.astype(bf16)
    if paired:
        beside = lax.ppermute(own, "scan", swap)
        whole = jnp.stack([by_slot(own, beside), by_slot(beside, own)])
        probe_pieces = [probe_wave, lax.ppermute(probe_wave, "scan", swap)]
    else:
        whole = lax.all_gather(own, "scan")
        every = lax.all_gather(probe_wave, "scan")
        probe_pieces = [every[number] for number in range(parts)]
    notes = brought(jnp.concatenate([row_offsets, position_counts]), -ahead)
    live = (slot < notes[slots]).astype(jnp.int32)
    core = lax.rem(lax.axis_index("tile"), 2)
    meta = jnp.stack(
        [notes[jnp.minimum(slot, slots - 1)], live, slot.astype(jnp.int32), core.astype(jnp.int32)]
    )
    if paired:
        amp_pieces = [
            lax.ppermute(
                by_slot(amplitudes[which], amplitudes[1 - which]).astype(bf16),
                ("tile", "scan"),
                [
                    ((home - ahead) * 2 + x, home * 2 + (x + which) % 2)
                    for home in homes
                    for x in range(2)
                ],
            )
            for which in range(2)
        ]
    else:
        every = lax.all_gather(brought(amplitudes.astype(bf16), -ahead), "scan")
        amp_pieces = [every[:, jnp.minimum(slot, slots - 1)].reshape((size, size))]
    far_rows, far_cols, near = tables(size)
    whole, meta = lax.optimization_barrier((whole, meta))
    turned = rolled(probe_pieces, amp_pieces, far_rows, far_cols, meta, size)
    steps = range(-ahead, ahead + 1, 2)
    kept, turned = lax.optimization_barrier((whole, turned))
    mine = jnp.stack([brought(whole, step) if step else kept for step in steps])
    theirs = to_partner(mine)
    keep, send = waves(mine, theirs, (far_rows, far_cols, near), turned, meta, size)
    merged = (keep.astype(f32) + to_partner(send).astype(f32)).astype(bf16)
    total = sum(
        (returned(merged[i], step) if step else merged[i]).astype(f32)
        for i, step in enumerate(steps)
    )
    if paired:
        away = lax.ppermute(by_slot(total[1], total[0]).astype(bf16), "scan", swap)
        return by_slot(total[0], total[1]) + away.astype(f32)
    return lax.psum_scatter(total, "scan", scatter_dimension=0, tiled=False)


def solution(mesh):
    in_specs = (
        P(None, None, "tile", "scan"),
        P(None, None, "scan"),
        P("tile", "scan", None),
        P("tile"),
        P("tile"),
    )
    out_specs = P(None, None, "tile", "scan")

    def run(object_slab, *rest):
        return jax.shard_map(
            functools.partial(shards, object_slab.shape[3]),
            mesh=mesh, in_specs=in_specs, out_specs=out_specs, check_vma=False,
        )(object_slab, *rest)

    return run
```

time: 110 us -> 93.3 us (0.85)
  waiting for transfers between devices: 39.7 us -> 28.2 us
  local copies, waits for them, and re-layouts: 7.72 us -> 1.9 us
  starting transfers between devices: 35.1 us -> 40.2 us
  Pallas kernels: 18.7 us -> 14.5 us
    ppermute x1, waiting for transfers between devices: 10.3 us -> 0.01 us  [shards(): probe_pieces = [probe_wave, lax.ppermute(probe_wave, 'scan', swap)]]
    unnamed x21 -> x14, local copies, waits for them, and re-layouts: 6.27 us -> 1.14 us
    pallas_call x1, Pallas kernels: 15.7 us -> 11.8 us  [waves(): pl.pallas_call(functools.partial(wave_kernel, size, span, tile_rows), out...]
    ppermute x1, waiting for transfers between devices: 3.75 us -> 0.03 us  [shards(): beside = lax.ppermute(own, 'scan', swap)]
    ppermute x5, waiting for transfers between devices: 7.73 us -> 4.46 us  [brought(): return lax.ppermute(value, 'tile', [(home + steps, home) for home in homes])]
    ppermute x4, starting transfers between devices: 12 us -> 14.8 us  [returned(): return lax.ppermute(value, 'tile', [(home, home + steps) for home in homes])]
    ppermute x2, waiting for transfers between devices: 3.21 us -> 5.88 us  [to_partner(): return lax.ppermute(value, 'tile', [(home, home ^ 1) for home in homes])]
    ppermute x2, waiting for transfers between devices: 0.01 us -> 2.42 us  [shards(): lax.ppermute(by_slot(amplitudes[which], amplitudes[1 - which]).astype(bf1...]
  transfers between devices with their start and end apart: 16 -> 16, of which waited for: 10 -> 9; matrix products, arithmetic and copies ran while one was open for 4% -> 4% of each run, Pallas kernels for 3% -> 3%
where the time goes in v1:
time: 93.3 us; the launch traced here: 92.8 us
  starting transfers between devices  40.2 us (43%)
  waiting for transfers between devices  28.2 us (30%)
  Pallas kernels  14.5 us (16%)
  other arithmetic  6.27 us (7%)
  local copies, waits for them, and re-layouts  1.9 us (2%)
  between operations  1.68 us (2%)
    ppermute x4, starting transfers between devices, returned(): return lax.ppermute(value, 'tile', [(home, home + steps) for home in homes])  14.8 us
    ppermute x5, starting transfers between devices, brought(): return lax.ppermute(value, 'tile', [(home + steps, home) for home in homes])  14.2 us
    ppermute x4, waiting for transfers between devices, returned(): return lax.ppermute(value, 'tile', [(home, home + steps) for home in homes])  11.9 us
    pallas_call x1, Pallas kernels, waves(): pl.pallas_call(functools.partial(wave_kernel, size, span, tile_rows), out...  11.8 us
    ppermute x2, waiting for transfers between devices, to_partner(): return lax.ppermute(value, 'tile', [(home, home ^ 1) for home in homes])  5.88 us
    ppermute x5, waiting for transfers between devices, brought(): return lax.ppermute(value, 'tile', [(home + steps, home) for home in homes])  4.46 us
    ppermute x2, starting transfers between devices, to_partner(): return lax.ppermute(value, 'tile', [(home, home ^ 1) for home in homes])  3.96 us
    ppermute x1, waiting for transfers between devices, shards(): away = lax.ppermute(by_slot(total[1], total[0]).astype(bf16), 'scan', swap)  3.48 us
  transfers between devices with their start and end apart: 16, of which 9 were waited for; matrix products, arithmetic and copies ran while one was open for 4% of the time, Pallas kernels for 3%

profile of v1, /device:TPU:16, one launch (start us, length us, event | category | flops | bytes accessed | tf_op | source)
XLA Modules:
  0.0 92.8 jit_solution(5344329700958910723)
XLA Ops:
  1.4 1.3 %collective-permute-start.1 = (s32[3]{0:T(128)S(1)}, s32[3]{0:T(128)S(1)}, u32[]{:S(2)}, u32[]{:S(2)}) collective-permute-start(s32[3]{0:T(128)S(1)} %pad_add_fusion), channel_id=1, source_target_pairs={{0,8},{2,10},{4,12},{6,14},{8,16},{10,18},{12,20},{14,22},{1,9},{3... | collective-permute-start | bytes 44 | tf_op jit(solution)/shard_map/ppermute | solution.py:344
  2.7 1.0 %convert_element_type.52 = bf16[2,2,64,256]{3,2,1,0:T(8,128)(2,1)S(1)} convert(f32[2,2,64,256]{3,2,1,0:T(8,128)} %param.8) | non-fusion elementwise | flops 65536 | bytes 393216 | tf_op jit(solution)/shard_map/convert_element_type | solution.py:355
  3.7 1.6 %collective-permute-start = (bf16[2,2,64,256]{3,2,1,0:T(8,128)(2,1)S(1)}, bf16[2,2,64,256]{3,2,1,0:T(8,128)(2,1)S(1)}, u32[]{:S(2)}, u32[]{:S(2)}) collective-permute-start(bf16[2,2,64,256]{3,2,1,0:T(8,128)(2,1)S(1)} %convert_element_type.52), channel_id=1, source_target_pairs={{0,1},{1,0},{2,3},{3,2},{4,5},{5,4},{6,7},{7,6},{8,9},{9,8},{10,11... | collective-permute-start | bytes 393224 | tf_op jit(solution)/shard_map/ppermute | solution.py:357
  5.3 1.6 %collective-permute-done.1 = s32[3]{0:T(128)S(1)} collective-permute-done((s32[3]{0:T(128)S(1)}, s32[3]{0:T(128)S(1)}, u32[]{:S(2)}, u32[]{:S(2)}) %collective-permute-start.1) | collective-permute-done | bytes 44 | tf_op jit(solution)/shard_map/ppermute | solution.py:344
  9.0 1.1 %select_bitcast_fusion.1 = (bf16[1,2,2,64,256]{4,3,2,1,0:T(8,128)(2,1)S(1)}, bf16[1,2,2,64,256]{4,3,2,1,0:T(8,128)(2,1)S(1)}) fusion(bf16[2,2,64,256]{3,2,1,0:T(8,128)(2,1)S(1)} %collective-permute-done, pred[]{:T(512)S(6)} %eq.2, f32[2,2,64,256]{3,2,1,0:T(8,128)} %param.8), kind=kLoop, calls=%fused_computation.23 | loop fusion | flops 196608 | bytes 655361 | tf_op jit(solution)/shard_map/stack | solution.py:358
  10.2 1.4 %collective-permute-start.2 = (bf16[2,2,2,64,256]{4,3,2,1,0:T(8,128)(2,1)S(1)}, bf16[2,2,2,64,256]{4,3,2,1,0:T(8,128)(2,1)S(1)}, u32[]{:S(2)}, u32[]{:S(2)}) collective-permute-start(bf16[2,2,2,64,256]{4,3,2,1,0:T(8,128)(2,1)S(1)} %pad_maximum_fusion), channel_id=1, source_target_pairs={{0,8},{2,10},{4,12},{6,14},{8,16},{10,18},{12,20},{14,22},{1,9},{3... | collective-permute-start | bytes 786440 | tf_op jit(solution)/shard_map/ppermute | solution.py:344
  11.6 1.6 %collective-permute-start.4 = (bf16[2,512,256]{2,1,0:T(8,128)(2,1)S(1)}, bf16[2,512,256]{2,1,0:T(8,128)(2,1)S(1)}, u32[]{:S(2)}, u32[]{:S(2)}) collective-permute-start(bf16[2,512,256]{2,1,0:T(8,128)(2,1)S(1)} %copy-done), channel_id=1, source_target_pairs={{0,1},{1,0},{2,3},{3,2},{4,5},{5,4},{6,7},{7,6},{8,9},{9,8},{10,11... | collective-permute-start | bytes 1572872 | tf_op jit(solution)/shard_map/ppermute | solution.py:359
  13.2 3.4 %collective-permute-start.3 = (bf16[2,2,2,64,256]{4,3,2,1,0:T(8,128)(2,1)S(1)}, bf16[2,2,2,64,256]{4,3,2,1,0:T(8,128)(2,1)S(1)}, u32[]{:S(2)}, u32[]{:S(2)}) collective-permute-start(bf16[2,2,2,64,256]{4,3,2,1,0:T(8,128)(2,1)S(1)} %pad_maximum_fusion), channel_id=1, source_target_pairs={{4,8},{6,10},{8,12},{10,14},{12,16},{14,18},{16,20},{18,22},{5,9},... | collective-permute-start | bytes 786440 | tf_op jit(solution)/shard_map/ppermute | solution.py:344
  16.6 1.3 %fusion.3 = (bf16[256,512]{1,0:T(8,128)(2,1)S(1)}, bf16[256,512]{1,0:T(8,128)(2,1)S(1)}) fusion(f32[2,256,512]{2,1,0:T(8,128)} %param.10, pred[]{:T(512)S(6)} %eq.2), kind=kLoop, calls=%fused_computation.7 | loop fusion | flops 262144 | bytes 1048577 | tf_op jit(solution)/shard_map/convert_element_type | solution.py:373
  17.8 1.3 %collective-permute-start.6 = (bf16[256,512]{1,0:T(8,128)(2,1)S(1)}, bf16[256,512]{1,0:T(8,128)(2,1)S(1)}, u32[]{:S(2)}, u32[]{:S(2)}) collective-permute-start(bf16[256,512]{1,0:T(8,128)(2,1)S(1)} %get-tuple-element.35), channel_id=1, source_target_pairs={{0,9},{1,8},{2,11},{3,10},{4,13},{5,12},{6,15},{7,14},{8,17},{9,16... | collective-permute-start | bytes 786440 | tf_op jit(solution)/shard_map/ppermute | solution.py:372
  19.1 1.3 %collective-permute-start.5 = (bf16[256,512]{1,0:T(8,128)(2,1)S(1)}, bf16[256,512]{1,0:T(8,128)(2,1)S(1)}, u32[]{:S(2)}, u32[]{:S(2)}) collective-permute-start(bf16[256,512]{1,0:T(8,128)(2,1)S(1)} %get-tuple-element.36), channel_id=1, source_target_pairs={{0,8},{1,9},{2,10},{3,11},{4,12},{5,13},{6,14},{7,15},{8,16},{9,17... | collective-permute-start | bytes 786440 | tf_op jit(solution)/shard_map/ppermute | solution.py:372
  20.4 6.2 %collective-permute-start.8 = (bf16[2,2,2,64,256]{4,3,2,1,0:T(8,128)(2,1)S(1)}, bf16[2,2,2,64,256]{4,3,2,1,0:T(8,128)(2,1)S(1)}, u32[]{:S(2)}, u32[]{:S(2)}) collective-permute-start(bf16[2,2,2,64,256]{4,3,2,1,0:T(8,128)(2,1)S(1)} %pad_maximum_fusion), channel_id=1, source_target_pairs={{16,8},{18,10},{20,12},{22,14},{24,16},{26,18},{28,20},{30,22},{17... | collective-permute-start | bytes 786440 | tf_op jit(solution)/shard_map/ppermute | solution.py:344
  26.7 1.7 %collective-permute-done.3 = bf16[2,2,2,64,256]{4,3,2,1,0:T(8,128)(2,1)S(1)} collective-permute-done((bf16[2,2,2,64,256]{4,3,2,1,0:T(8,128)(2,1)S(1)}, bf16[2,2,2,64,256]{4,3,2,1,0:T(8,128)(2,1)S(1)}, u32[]{:S(2)}, u32[]{:S(2)}) %collective-permute-start.3) | collective-permute-done | bytes 262176 | tf_op jit(solution)/shard_map/ppermute | solution.py:344
  28.4 1.9 %collective-permute-start.7 = (bf16[2,2,2,64,256]{4,3,2,1,0:T(8,128)(2,1)S(1)}, bf16[2,2,2,64,256]{4,3,2,1,0:T(8,128)(2,1)S(1)}, u32[]{:S(2)}, u32[]{:S(2)}) collective-permute-start(bf16[2,2,2,64,256]{4,3,2,1,0:T(8,128)(2,1)S(1)} %pad_maximum_fusion), channel_id=1, source_target_pairs={{12,8},{14,10},{16,12},{18,14},{20,16},{22,18},{24,20},{26,22},{13... | collective-permute-start | bytes 786440 | tf_op jit(solution)/shard_map/ppermute | solution.py:344
  30.3 2.4 %collective-permute-done.5.refs_2_ = bf16[256,512]{1,0:T(8,128)(2,1)S(1)} collective-permute-done((bf16[256,512]{1,0:T(8,128)(2,1)S(1)}, bf16[256,512]{1,0:T(8,128)(2,1)S(1)}, u32[]{:S(2)}, u32[]{:S(2)}) %collective-permute-start.5) | collective-permute-done | bytes 262176 | tf_op jit(solution)/shard_map/ppermute | solution.py:372
  32.7 2.7 %rolled.1 = (bf16[2,512,512]{2,1,0:T(8,128)(2,1)S(1)}, bf16[3,512,256]{2,1,0:T(8,128)(2,1)S(1)}, bf16[3,256,512]{2,1,0:T(8,128)(2,1)S(1)}, bf16[512,512]{1,0:T(8,128)(2,1)S(1)}) custom-call(s32[4]{0:T(128)S(1)} %pad_add_fusion.1.meta, bf16[3,512,512]{2,1,0:T(8,128)(2,1)S(1)} %copy-done.2, bf16[3,512,512]{2,1,0:T(8,128)(2,1)S(1)} %copy-done.1, ...), custom_call_target="tpu_custom_call" | custom-call | flops 8589934592 | bytes 6291456 | tf_op jit(solution)/shard_map/rolled/pallas_call | solution.py:109
  35.5 1.1 %collective-permute-done.7 = bf16[2,2,2,64,256]{4,3,2,1,0:T(8,128)(2,1)S(1)} collective-permute-done((bf16[2,2,2,64,256]{4,3,2,1,0:T(8,128)(2,1)S(1)}, bf16[2,2,2,64,256]{4,3,2,1,0:T(8,128)(2,1)S(1)}, u32[]{:S(2)}, u32[]{:S(2)}) %collective-permute-start.7) | collective-permute-done | bytes 262176 | tf_op jit(solution)/shard_map/ppermute | solution.py:344
  36.7 1.9 %collective-permute-start.9 = (bf16[5,2,2,2,64,256]{5,4,3,2,1,0:T(8,128)(2,1)S(1)}, bf16[5,2,2,2,64,256]{5,4,3,2,1,0:T(8,128)(2,1)S(1)}, u32[]{:S(2)}, u32[]{:S(2)}) collective-permute-start(bf16[5,2,2,2,64,256]{5,4,3,2,1,0:T(8,128)(2,1)S(1)} %bitcast_dynamic-update-slice_fusion.mine), channel_id=1, source_target_pairs={{8,10},{10,8},{12,14},{14,12},{16,18},{18,16},{20,22},{22,20},{9,1... | collective-permute-start | bytes 3932168 | tf_op jit(solution)/shard_map/ppermute | solution.py:350
  38.6 3.0 %collective-permute-done.9.theirs = bf16[5,2,2,2,64,256]{5,4,3,2,1,0:T(8,128)(2,1)S(1)} collective-permute-done((bf16[5,2,2,2,64,256]{5,4,3,2,1,0:T(8,128)(2,1)S(1)}, bf16[5,2,2,2,64,256]{5,4,3,2,1,0:T(8,128)(2,1)S(1)}, u32[]{:S(2)}, u32[]{:S(2)}) %collective-permute-start.9) | collective-permute-done | bytes 1310752 | tf_op jit(solution)/shard_map/ppermute | solution.py:350
  41.6 1.0 %copy-done.4 = bf16[5,2,2,2,64,256]{5,4,3,2,1,0:T(8,128)(2,1)} copy-done((bf16[5,2,2,2,64,256]{5,4,3,2,1,0:T(8,128)(2,1)}, bf16[5,2,2,2,64,256]{5,4,3,2,1,0:T(8,128)(2,1)S(1)}, u32[]{:S(2)}) %copy-start.4) | copy-done | bytes 1310744
  42.7 11.8 %waves.1 = (bf16[5,2,2,2,64,256]{5,4,3,2,1,0:T(8,128)(2,1)S(1)}, bf16[5,2,2,2,64,256]{5,4,3,2,1,0:T(8,128)(2,1)S(1)}) custom-call(s32[4]{0:T(128)S(1)} %pad_add_fusion.1.meta, bf16[5,2,2,2,64,256]{5,4,3,2,1,0:T(8,128)(2,1)} %copy-done.3, bf16[5,2,2,2,64,256]{5,4,3,2,1,0:T(8,128)(2,1)} %copy-done.4, ...), custom_call_target="tpu_custom_call" | custom-call | flops 8589934592 | bytes 6291456 | tf_op jit(solution)/shard_map/waves/pallas_call | solution.py:304
  54.5 2.0 %collective-permute-start.10 = (bf16[5,2,2,2,64,256]{5,4,3,2,1,0:T(8,128)(2,1)S(1)}, bf16[5,2,2,2,64,256]{5,4,3,2,1,0:T(8,128)(2,1)S(1)}, u32[]{:S(2)}, u32[]{:S(2)}) collective-permute-start(bf16[5,2,2,2,64,256]{5,4,3,2,1,0:T(8,128)(2,1)S(1)} %get-tuple-element.30), channel_id=1, source_target_pairs={{8,10},{10,8},{12,14},{14,12},{16,18},{18,16},{20,22},{22,20},{9,1... | collective-permute-start | bytes 3932168 | tf_op jit(solution)/shard_map/ppermute | solution.py:350
  56.6 2.9 %collective-permute-done.10 = bf16[5,2,2,2,64,256]{5,4,3,2,1,0:T(8,128)(2,1)S(1)} collective-permute-done((bf16[5,2,2,2,64,256]{5,4,3,2,1,0:T(8,128)(2,1)S(1)}, bf16[5,2,2,2,64,256]{5,4,3,2,1,0:T(8,128)(2,1)S(1)}, u32[]{:S(2)}, u32[]{:S(2)}) %collective-permute-start.10) | collective-permute-done | bytes 1310752 | tf_op jit(solution)/shard_map/ppermute | solution.py:350
  60.0 3.8 %collective-permute-start.11 = (bf16[2,2,2,64,256]{4,3,2,1,0:T(8,128)(2,1)S(1)}, bf16[2,2,2,64,256]{4,3,2,1,0:T(8,128)(2,1)S(1)}, u32[]{:S(2)}, u32[]{:S(2)}) collective-permute-start(bf16[2,2,2,64,256]{4,3,2,1,0:T(8,128)(2,1)S(1)} %get-tuple-element.31), channel_id=1, source_target_pairs={{8,0},{10,2},{12,4},{14,6},{16,8},{18,10},{20,12},{22,14},{9,1},{1... | collective-permute-start | bytes 786440 | tf_op jit(solution)/shard_map/ppermute | solution.py:347
  63.8 1.9 %collective-permute-start.14 = (bf16[2,2,2,64,256]{4,3,2,1,0:T(8,128)(2,1)S(1)}, bf16[2,2,2,64,256]{4,3,2,1,0:T(8,128)(2,1)S(1)}, u32[]{:S(2)}, u32[]{:S(2)}) collective-permute-start(bf16[2,2,2,64,256]{4,3,2,1,0:T(8,128)(2,1)S(1)} %get-tuple-element.32), channel_id=1, source_target_pairs={{8,16},{10,18},{12,20},{14,22},{16,24},{18,26},{20,28},{22,30},{9,... | collective-permute-start | bytes 786440 | tf_op jit(solution)/shard_map/ppermute | solution.py:347
  65.7 5.8 %collective-permute-start.13 = (bf16[2,2,2,64,256]{4,3,2,1,0:T(8,128)(2,1)S(1)}, bf16[2,2,2,64,256]{4,3,2,1,0:T(8,128)(2,1)S(1)}, u32[]{:S(2)}, u32[]{:S(2)}) collective-permute-start(bf16[2,2,2,64,256]{4,3,2,1,0:T(8,128)(2,1)S(1)} %get-tuple-element.33), channel_id=1, source_target_pairs={{8,12},{10,14},{12,16},{14,18},{16,20},{18,22},{20,24},{22,26},{9,... | collective-permute-start | bytes 786440 | tf_op jit(solution)/shard_map/ppermute | solution.py:347
  71.5 3.4 %collective-permute-start.12 = (bf16[2,2,2,64,256]{4,3,2,1,0:T(8,128)(2,1)S(1)}, bf16[2,2,2,64,256]{4,3,2,1,0:T(8,128)(2,1)S(1)}, u32[]{:S(2)}, u32[]{:S(2)}) collective-permute-start(bf16[2,2,2,64,256]{4,3,2,1,0:T(8,128)(2,1)S(1)} %get-tuple-element.34), channel_id=1, source_target_pairs={{8,4},{10,6},{12,8},{14,10},{16,12},{18,14},{20,16},{22,18},{9,5},... | collective-permute-start | bytes 786440 | tf_op jit(solution)/shard_map/ppermute | solution.py:347
  74.9 7.9 %collective-permute-done.13 = bf16[2,2,2,64,256]{4,3,2,1,0:T(8,128)(2,1)S(1)} collective-permute-done((bf16[2,2,2,64,256]{4,3,2,1,0:T(8,128)(2,1)S(1)}, bf16[2,2,2,64,256]{4,3,2,1,0:T(8,128)(2,1)S(1)}, u32[]{:S(2)}, u32[]{:S(2)}) %collective-permute-start.13) | collective-permute-done | bytes 262176 | tf_op jit(solution)/shard_map/ppermute | solution.py:347
  82.8 4.0 %collective-permute-done.12 = bf16[2,2,2,64,256]{4,3,2,1,0:T(8,128)(2,1)S(1)} collective-permute-done((bf16[2,2,2,64,256]{4,3,2,1,0:T(8,128)(2,1)S(1)}, bf16[2,2,2,64,256]{4,3,2,1,0:T(8,128)(2,1)S(1)}, u32[]{:S(2)}, u32[]{:S(2)}) %collective-permute-start.12) | collective-permute-done | bytes 262176 | tf_op jit(solution)/shard_map/ppermute | solution.py:347
  87.0 1.6 %collective-permute-start.15 = (bf16[2,2,64,256]{3,2,1,0:T(8,128)(2,1)S(1)}, bf16[2,2,64,256]{3,2,1,0:T(8,128)(2,1)S(1)}, u32[]{:S(2)}, u32[]{:S(2)}) collective-permute-start(bf16[2,2,64,256]{3,2,1,0:T(8,128)(2,1)S(1)} %fusion.4), channel_id=1, source_target_pairs={{0,1},{1,0},{2,3},{3,2},{4,5},{5,4},{6,7},{7,6},{8,9},{9,8},{10,11... | collective-permute-start | bytes 393224 | tf_op jit(solution)/shard_map/ppermute | solution.py:400
  88.5 3.5 %collective-permute-done.15 = bf16[2,2,64,256]{3,2,1,0:T(8,128)(2,1)S(1)} collective-permute-done((bf16[2,2,64,256]{3,2,1,0:T(8,128)(2,1)S(1)}, bf16[2,2,64,256]{3,2,1,0:T(8,128)(2,1)S(1)}, u32[]{:S(2)}, u32[]{:S(2)}) %collective-permute-start.15) | collective-permute-done | bytes 131104 | tf_op jit(solution)/shard_map/ppermute | solution.py:400
  92.0 0.8 bitcast_add_fusion
  (29 shorter events, 3.1 us)
Async XLA Ops:
  0.0 11.6 %copy-start = (bf16[2,512,256]{2,1,0:T(8,128)(2,1)S(1)}, bf16[2,512,256]{2,1,0:T(8,128)(2,1)}, u32[]{:S(2)}) copy-start(bf16[2,512,256]{2,1,0:T(8,128)(2,1)} %refs_0_.1) | copy-start | bytes 1572868
  1.4 5.4 %collective-permute-start.1 = (s32[3]{0:T(128)S(1)}, s32[3]{0:T(128)S(1)}, u32[]{:S(2)}, u32[]{:S(2)}) collective-permute-start(s32[3]{0:T(128)S(1)} %pad_add_fusion), channel_id=1, source_target_pairs={{0,8},{2,10},{4,12},{6,14},{8,16},{10,18},{12,20},{14,22},{1,9},{3... | collective-permute-start | bytes 44 | tf_op jit(solution)/shard_map/ppermute | solution.py:344
  3.7 5.3 %collective-permute-start = (bf16[2,2,64,256]{3,2,1,0:T(8,128)(2,1)S(1)}, bf16[2,2,64,256]{3,2,1,0:T(8,128)(2,1)S(1)}, u32[]{:S(2)}, u32[]{:S(2)}) collective-permute-start(bf16[2,2,64,256]{3,2,1,0:T(8,128)(2,1)S(1)} %convert_element_type.52), channel_id=1, source_target_pairs={{0,1},{1,0},{2,3},{3,2},{4,5},{5,4},{6,7},{7,6},{8,9},{9,8},{10,11... | collective-permute-start | bytes 393224 | tf_op jit(solution)/shard_map/ppermute | solution.py:357
  9.0 23.7 %copy-start.2 = (bf16[3,512,512]{2,1,0:T(8,128)(2,1)S(1)}, bf16[3,512,512]{2,1,0:T(8,128)(2,1)}, u32[]{:S(2)}) copy-start(bf16[3,512,512]{2,1,0:T(8,128)(2,1)} %constant.23.clone.far_rows.far_rows_hbm) | copy-start | bytes 4718596
  10.1 22.6 %copy-start.1 = (bf16[3,512,512]{2,1,0:T(8,128)(2,1)S(1)}, bf16[3,512,512]{2,1,0:T(8,128)(2,1)}, u32[]{:S(2)}) copy-start(bf16[3,512,512]{2,1,0:T(8,128)(2,1)} %constant.24.clone.far_cols.far_cols_hbm) | copy-start | bytes 4718596
  10.2 10.3 %collective-permute-start.2 = (bf16[2,2,2,64,256]{4,3,2,1,0:T(8,128)(2,1)S(1)}, bf16[2,2,2,64,256]{4,3,2,1,0:T(8,128)(2,1)S(1)}, u32[]{:S(2)}, u32[]{:S(2)}) collective-permute-start(bf16[2,2,2,64,256]{4,3,2,1,0:T(8,128)(2,1)S(1)} %pad_maximum_fusion), channel_id=1, source_target_pairs={{0,8},{2,10},{4,12},{6,14},{8,16},{10,18},{12,20},{14,22},{1,9},{3... | collective-permute-start | bytes 786440 | tf_op jit(solution)/shard_map/ppermute | solution.py:344
  11.6 21.1 %collective-permute-start.4 = (bf16[2,512,256]{2,1,0:T(8,128)(2,1)S(1)}, bf16[2,512,256]{2,1,0:T(8,128)(2,1)S(1)}, u32[]{:S(2)}, u32[]{:S(2)}) collective-permute-start(bf16[2,512,256]{2,1,0:T(8,128)(2,1)S(1)} %copy-done), channel_id=1, source_target_pairs={{0,1},{1,0},{2,3},{3,2},{4,5},{5,4},{6,7},{7,6},{8,9},{9,8},{10,11... | collective-permute-start | bytes 1572872 | tf_op jit(solution)/shard_map/ppermute | solution.py:359
  13.2 15.2 %collective-permute-start.3 = (bf16[2,2,2,64,256]{4,3,2,1,0:T(8,128)(2,1)S(1)}, bf16[2,2,2,64,256]{4,3,2,1,0:T(8,128)(2,1)S(1)}, u32[]{:S(2)}, u32[]{:S(2)}) collective-permute-start(bf16[2,2,2,64,256]{4,3,2,1,0:T(8,128)(2,1)S(1)} %pad_maximum_fusion), channel_id=1, source_target_pairs={{4,8},{6,10},{8,12},{10,14},{12,16},{14,18},{16,20},{18,22},{5,9},... | collective-permute-start | bytes 786440 | tf_op jit(solution)/shard_map/ppermute | solution.py:344
  17.8 12.5 %collective-permute-start.6 = (bf16[256,512]{1,0:T(8,128)(2,1)S(1)}, bf16[256,512]{1,0:T(8,128)(2,1)S(1)}, u32[]{:S(2)}, u32[]{:S(2)}) collective-permute-start(bf16[256,512]{1,0:T(8,128)(2,1)S(1)} %get-tuple-element.35), channel_id=1, source_target_pairs={{0,9},{1,8},{2,11},{3,10},{4,13},{5,12},{6,15},{7,14},{8,17},{9,16... | collective-permute-start | bytes 786440 | tf_op jit(solution)/shard_map/ppermute | solution.py:372
  19.1 13.6 %collective-permute-start.5 = (bf16[256,512]{1,0:T(8,128)(2,1)S(1)}, bf16[256,512]{1,0:T(8,128)(2,1)S(1)}, u32[]{:S(2)}, u32[]{:S(2)}) collective-permute-start(bf16[256,512]{1,0:T(8,128)(2,1)S(1)} %get-tuple-element.36), channel_id=1, source_target_pairs={{0,8},{1,9},{2,10},{3,11},{4,12},{5,13},{6,14},{7,15},{8,16},{9,17... | collective-permute-start | bytes 786440 | tf_op jit(solution)/shard_map/ppermute | solution.py:372
  20.4 16.2 %collective-permute-start.8 = (bf16[2,2,2,64,256]{4,3,2,1,0:T(8,128)(2,1)S(1)}, bf16[2,2,2,64,256]{4,3,2,1,0:T(8,128)(2,1)S(1)}, u32[]{:S(2)}, u32[]{:S(2)}) collective-permute-start(bf16[2,2,2,64,256]{4,3,2,1,0:T(8,128)(2,1)S(1)} %pad_maximum_fusion), channel_id=1, source_target_pairs={{16,8},{18,10},{20,12},{22,14},{24,16},{26,18},{28,20},{30,22},{17... | collective-permute-start | bytes 786440 | tf_op jit(solution)/shard_map/ppermute | solution.py:344
  28.4 8.3 %collective-permute-start.7 = (bf16[2,2,2,64,256]{4,3,2,1,0:T(8,128)(2,1)S(1)}, bf16[2,2,2,64,256]{4,3,2,1,0:T(8,128)(2,1)S(1)}, u32[]{:S(2)}, u32[]{:S(2)}) collective-permute-start(bf16[2,2,2,64,256]{4,3,2,1,0:T(8,128)(2,1)S(1)} %pad_maximum_fusion), channel_id=1, source_target_pairs={{12,8},{14,10},{16,12},{18,14},{20,16},{22,18},{24,20},{26,22},{13... | collective-permute-start | bytes 786440 | tf_op jit(solution)/shard_map/ppermute | solution.py:344
  36.7 4.9 %copy-start.3 = (bf16[5,2,2,2,64,256]{5,4,3,2,1,0:T(8,128)(2,1)}, bf16[5,2,2,2,64,256]{5,4,3,2,1,0:T(8,128)(2,1)S(1)}, u32[]{:S(2)}) copy-start(bf16[5,2,2,2,64,256]{5,4,3,2,1,0:T(8,128)(2,1)S(1)} %bitcast_dynamic-update-slice_fusion.mine) | copy-start | bytes 3932164
  36.7 4.9 %collective-permute-start.9 = (bf16[5,2,2,2,64,256]{5,4,3,2,1,0:T(8,128)(2,1)S(1)}, bf16[5,2,2,2,64,256]{5,4,3,2,1,0:T(8,128)(2,1)S(1)}, u32[]{:S(2)}, u32[]{:S(2)}) collective-permute-start(bf16[5,2,2,2,64,256]{5,4,3,2,1,0:T(8,128)(2,1)S(1)} %bitcast_dynamic-update-slice_fusion.mine), channel_id=1, source_target_pairs={{8,10},{10,8},{12,14},{14,12},{16,18},{18,16},{20,22},{22,20},{9,1... | collective-permute-start | bytes 3932168 | tf_op jit(solution)/shard_map/ppermute | solution.py:350
  41.6 1.1 %copy-start.4 = (bf16[5,2,2,2,64,256]{5,4,3,2,1,0:T(8,128)(2,1)}, bf16[5,2,2,2,64,256]{5,4,3,2,1,0:T(8,128)(2,1)S(1)}, u32[]{:S(2)}) copy-start(bf16[5,2,2,2,64,256]{5,4,3,2,1,0:T(8,128)(2,1)S(1)} %collective-permute-done.9.theirs) | copy-start | bytes 3932164
  54.5 4.9 %collective-permute-start.10 = (bf16[5,2,2,2,64,256]{5,4,3,2,1,0:T(8,128)(2,1)S(1)}, bf16[5,2,2,2,64,256]{5,4,3,2,1,0:T(8,128)(2,1)S(1)}, u32[]{:S(2)}, u32[]{:S(2)}) collective-permute-start(bf16[5,2,2,2,64,256]{5,4,3,2,1,0:T(8,128)(2,1)S(1)} %get-tuple-element.30), channel_id=1, source_target_pairs={{8,10},{10,8},{12,14},{14,12},{16,18},{18,16},{20,22},{22,20},{9,1... | collective-permute-start | bytes 3932168 | tf_op jit(solution)/shard_map/ppermute | solution.py:350
  60.0 14.9 %collective-permute-start.11 = (bf16[2,2,2,64,256]{4,3,2,1,0:T(8,128)(2,1)S(1)}, bf16[2,2,2,64,256]{4,3,2,1,0:T(8,128)(2,1)S(1)}, u32[]{:S(2)}, u32[]{:S(2)}) collective-permute-start(bf16[2,2,2,64,256]{4,3,2,1,0:T(8,128)(2,1)S(1)} %get-tuple-element.31), channel_id=1, source_target_pairs={{8,0},{10,2},{12,4},{14,6},{16,8},{18,10},{20,12},{22,14},{9,1},{1... | collective-permute-start | bytes 786440 | tf_op jit(solution)/shard_map/ppermute | solution.py:347
  63.8 11.1 %collective-permute-start.14 = (bf16[2,2,2,64,256]{4,3,2,1,0:T(8,128)(2,1)S(1)}, bf16[2,2,2,64,256]{4,3,2,1,0:T(8,128)(2,1)S(1)}, u32[]{:S(2)}, u32[]{:S(2)}) collective-permute-start(bf16[2,2,2,64,256]{4,3,2,1,0:T(8,128)(2,1)S(1)} %get-tuple-element.32), channel_id=1, source_target_pairs={{8,16},{10,18},{12,20},{14,22},{16,24},{18,26},{20,28},{22,30},{9,... | collective-permute-start | bytes 786440 | tf_op jit(solution)/shard_map/ppermute | solution.py:347
  65.7 17.0 %collective-permute-start.13 = (bf16[2,2,2,64,256]{4,3,2,1,0:T(8,128)(2,1)S(1)}, bf16[2,2,2,64,256]{4,3,2,1,0:T(8,128)(2,1)S(1)}, u32[]{:S(2)}, u32[]{:S(2)}) collective-permute-start(bf16[2,2,2,64,256]{4,3,2,1,0:T(8,128)(2,1)S(1)} %get-tuple-element.33), channel_id=1, source_target_pairs={{8,12},{10,14},{12,16},{14,18},{16,20},{18,22},{20,24},{22,26},{9,... | collective-permute-start | bytes 786440 | tf_op jit(solution)/shard_map/ppermute | solution.py:347
  71.5 15.3 %collective-permute-start.12 = (bf16[2,2,2,64,256]{4,3,2,1,0:T(8,128)(2,1)S(1)}, bf16[2,2,2,64,256]{4,3,2,1,0:T(8,128)(2,1)S(1)}, u32[]{:S(2)}, u32[]{:S(2)}) collective-permute-start(bf16[2,2,2,64,256]{4,3,2,1,0:T(8,128)(2,1)S(1)} %get-tuple-element.34), channel_id=1, source_target_pairs={{8,4},{10,6},{12,8},{14,10},{16,12},{18,14},{20,16},{22,18},{9,5},... | collective-permute-start | bytes 786440 | tf_op jit(solution)/shard_map/ppermute | solution.py:347
  87.0 5.0 %collective-permute-start.15 = (bf16[2,2,64,256]{3,2,1,0:T(8,128)(2,1)S(1)}, bf16[2,2,64,256]{3,2,1,0:T(8,128)(2,1)S(1)}, u32[]{:S(2)}, u32[]{:S(2)}) collective-permute-start(bf16[2,2,64,256]{3,2,1,0:T(8,128)(2,1)S(1)} %fusion.4), channel_id=1, source_target_pairs={{0,1},{1,0},{2,3},{3,2},{4,5},{5,4},{6,7},{7,6},{8,9},{9,8},{10,11... | collective-permute-start | bytes 393224 | tf_op jit(solution)/shard_map/ppermute | solution.py:400
